TPU v7x, 32 devices: a whole 2x2x4 slice. The times are simulated.
32 devices in a mesh: groups: 2 (over x), ep: 16 (over z, y, core).
Axes of the slice: x: 2, y: 2, z: 4, core: 2. Of those that a mesh axis runs over, the one named last changes fastest.
Arguments:
- thinker_rows: bfloat16 [512, 2048], P(('groups', 'ep')), parts along dimension 0, may hold values from -6 to 6
- expert_ids: int32 [512, 8], P(('groups', 'ep')), parts along dimension 0, may hold values from 0 to 15, all different within a row; in each aligned block of 16 rows (0 to 15, 16 to 31, ...) at most 16 rows name the same one
- gate_weights: float32 [512, 8], P(('groups', 'ep')), parts along dimension 0, may hold values from 0.2 to 1
- w_gate: bfloat16 [16, 2048, 512], P('ep'), may hold values from -0.125 to 0.125
- w_up: bfloat16 [16, 2048, 512], P('ep'), may hold values from -0.125 to 0.125
- w_down: bfloat16 [16, 512, 2048], P('ep'), may hold values from -0.25 to 0.25
- talker_proj: bfloat16 [2048, 1024], replicated, may hold values from -0.125 to 0.125
- talker_slot: int32 [32, 16], P(('groups', 'ep')), parts along dimension 0, may hold values from 0 to 15, each once within a row
- speech_count: int32 [512], P(('groups', 'ep')), parts along dimension 0, may hold values from 0 to 4
- left_context: bfloat16 [512, 6, 1024], P(('groups', 'ep')), parts along dimension 0, may hold values from -6 to 6
- frame_offset: float32 [4, 1024], replicated, may hold values from -6 to 6
- conv_weight: float32 [7, 1024], replicated, may hold values from -2.4 to 2.4
Outputs:
- voice_frames: bfloat16 [512, 4, 1024], P(('groups', 'ep')), parts along dimension 0
There are 2 independent parts, one for each index of `groups`. A program takes and returns all parts, laid end to end along the dimension named above; an argument that names none is the same for every part. Nothing has to cross between parts.
Inputs may be any that keep to these rules, and one draw needn't show every extreme that they name: `expert_ids`: each row names 8 different experts; among the rows of one device no expert is named by more than 16 rows, and in every draw some expert is named by exactly 16 rows of some device. `talker_slot`: each device's row is a permutation of 0 to 15.
All inputs are finite; a program needn't handle non-finite values.
Results may differ from a plain program's by a relative error of at most 0.007.
Values may be sent and summed in bfloat16 or wider, within the bound.
A program may use at most 64 MiB of HBM per device.

v0:
```python
import jax
import jax.numpy as jnp
from jax import lax
from jax.sharding import PartitionSpec as P

CAP = 16


def expert_block(block_rows, gate_mat, up_mat, down_mat):
    gate_act = jnp.dot(block_rows, gate_mat, preferred_element_type=jnp.float32)
    up_act = jnp.dot(block_rows, up_mat, preferred_element_type=jnp.float32)
    inner = (jax.nn.silu(gate_act) * up_act).astype(jnp.bfloat16)
    return jnp.dot(inner, down_mat, preferred_element_type=jnp.float32).astype(jnp.bfloat16)


def project(hidden, talker_proj):
    values = hidden.astype(jnp.float32)
    scaled = values * lax.rsqrt(jnp.mean(values * values, axis=-1, keepdims=True) + 1e-06)
    return jnp.dot(
        scaled.astype(jnp.bfloat16), talker_proj, preferred_element_type=jnp.float32
    ).astype(jnp.bfloat16)


def vocode(owned, speech_count, left_context, frame_offset, conv_weight):
    frames = owned.astype(jnp.float32)[:, None, :] + frame_offset[None, :, :]
    sequence = jnp.concatenate([left_context.astype(jnp.float32), frames], axis=1)
    taps = conv_weight.shape[0]
    horizon = frame_offset.shape[0]
    result = jnp.zeros_like(frames)
    for offset in range(taps):
        result = (
            result + conv_weight[offset][None, None, :] * sequence[:, offset : offset + horizon, :]
        )
    active = jnp.arange(horizon, dtype=jnp.int32)[None, :, None] < speech_count[:, None, None]
    return jnp.where(active, result, 0.0).astype(jnp.bfloat16)


def slot_positions(expert_ids, experts):
    flat_expert = expert_ids.reshape(-1)
    onehot = (flat_expert[:, None] == jnp.arange(experts, dtype=jnp.int32)[None, :]).astype(
        jnp.int32
    )
    position = jnp.sum((jnp.cumsum(onehot, axis=0) - onehot) * onehot, axis=1)
    return (flat_expert, position)


def run_and_return(buffer, w_gate, w_up, w_down):
    sources, slot_count, features = buffer.shape
    flattened = buffer.reshape(sources * slot_count, features)
    outputs = expert_block(flattened, w_gate[0], w_up[0], w_down[0]).reshape(
        sources, slot_count, features
    )
    return lax.all_to_all(outputs, "ep", split_axis=0, concat_axis=0, tiled=True)


def local(
    thinker_rows,
    expert_ids,
    gate_weights,
    w_gate,
    w_up,
    w_down,
    talker_proj,
    talker_slot,
    speech_count,
    left_context,
    frame_offset,
    conv_weight,
):
    devices = lax.axis_size("ep")
    streams_here, features = thinker_rows.shape
    chosen = expert_ids.shape[1]
    flat_expert, position = slot_positions(expert_ids, devices)
    row_index = jnp.arange(streams_here * chosen, dtype=jnp.int32) // chosen
    outgoing = (
        jnp.zeros((devices, CAP, features), jnp.bfloat16)
        .at[flat_expert, position]
        .set(thinker_rows[row_index])
    )
    returned = run_and_return(
        lax.all_to_all(outgoing, "ep", split_axis=0, concat_axis=0, tiled=True),
        w_gate,
        w_up,
        w_down,
    )
    lookup = (
        returned[flat_expert, position].astype(jnp.float32).reshape(streams_here, chosen, features)
    )
    mixture = jnp.sum(gate_weights[:, :, None] * lookup, axis=1)
    hidden = (thinker_rows.astype(jnp.float32) + mixture).astype(jnp.bfloat16)
    slots = talker_slot[0]
    per_owner = streams_here // devices
    talker_rows = project(hidden, talker_proj)
    placed = (
        jnp.zeros_like(talker_rows)
        .at[slots]
        .set(talker_rows)
        .reshape(devices, per_owner, talker_rows.shape[1])
    )
    owned = lax.all_to_all(placed, "ep", split_axis=0, concat_axis=0, tiled=True).reshape(
        streams_here, talker_rows.shape[1]
    )
    return vocode(owned, speech_count, left_context, frame_offset, conv_weight)


def solution(mesh):
    in_specs = (
        P(("groups", "ep"), None),
        P(("groups", "ep"), None),
        P(("groups", "ep"), None),
        P("ep", None, None),
        P("ep", None, None),
        P("ep", None, None),
        P(),
        P(("groups", "ep"), None),
        P(("groups", "ep")),
        P(("groups", "ep"), None, None),
        P(),
        P(),
    )
    out_specs = P(("groups", "ep"), None, None)
    return jax.shard_map(local, mesh=mesh, in_specs=in_specs, out_specs=out_specs, check_vma=False)
```

profile of v0, /device:TPU:0, one launch (start us, length us, event | category | flops | bytes accessed | tf_op | source)
XLA Modules:
  0.0 112.0 jit_solution(6375094843688649843)
XLA Ops:
  0.0 0.9 copy.27
  1.2 0.2 reduce_window_sum.11
  1.4 0.2 select_reduce_fusion
  1.6 1.7 %gather_fusion = bf16[128,2048]{1,0:T(8,128)(2,1)} fusion(bf16[16,2048]{1,0:T(8,128)(2,1)S(1)} %copy-done.1, s32[1024]{0:T(1024)S(1)} %pad_clamp_fusion), kind=kCustom, calls=%fused_computation | custom fusion | bytes 1049088 | tf_op jit(solution)/shard_map/gather | solution.py:78
  3.3 0.1 broadcast_in_dim.14
  3.4 17.0 %scatter_fusion = bf16[16,16,2048]{2,1,0:T(8,128)(2,1)S(1)} fusion(bf16[16,16,2048]{2,1,0:T(8,128)(2,1)S(1)} %broadcast_in_dim.14, s32[128]{0:T(128)S(1)} %get-tuple-element.5, bf16[128,2048]{1,0:T(8,128)(2,1)} %gather_fusion), kind=kCustom, calls=%fused_computation.2 | custom fusion | bytes 1573888 | tf_op jit(solution)/shard_map/scatter | solution.py:78
  20.4 32.2 %all_to_all.15 = bf16[16,16,2048]{2,1,0:T(8,128)(2,1)S(1)} all-to-all(bf16[16,16,2048]{2,1,0:T(8,128)(2,1)S(1)} %scatter_fusion), channel_id=1, replica_groups=mesh['groups'=2,'ep'=16] {'ep'}, dimensions={0} | all-to-all | bytes 2097152 | tf_op jit(solution)/shard_map/all_to_all | solution.py:81
  52.6 1.0 copy-done.3
  53.6 0.7 fusion.3
  54.4 4.3 %convolution_convert_fusion = bf16[256,2048]{1,0:T(8,128)(2,1)} fusion(bf16[1,512,2048]{2,1,0:T(8,128)(2,1)S(1)} %copy-done, bf16[256,2048]{1,0:T(8,128)(2,1)} %bitcast.53, bf16[1,2048,512]{2,1,0:T(8,128)(2,1)} %param.16, f32[256,512]{1,0:T(8,128)S(1)} %fusion.3), kind=kOutput, calls=%fused_computation.4 | convolution fusion | flops 1075052544 | bytes 6815744 | tf_op jit(solution)/shard_map/dot_general | solution.py:13
  58.7 5.1 %all-to-all-start.1 = ((bf16[16,16,2048]{2,1,0:T(8,128)(2,1)}), bf16[16,16,2048]{2,1,0:T(8,128)(2,1)S(1)}, u32[]{:S(2)}, u32[]{:S(2)}) async-start(bf16[16,16,2048]{2,1,0:T(8,128)(2,1)} %bitcast.51), calls=%async_computation.1 | async-start | bytes 2097152 | tf_op jit(solution)/shard_map/all_to_all | solution.py:53
  63.9 0.9 copy_convert_fusion
  64.9 21.9 %all-to-all-done.1 = bf16[16,16,2048]{2,1,0:T(8,128)(2,1)S(1)} async-done(((bf16[16,16,2048]{2,1,0:T(8,128)(2,1)}), bf16[16,16,2048]{2,1,0:T(8,128)(2,1)S(1)}, u32[]{:S(2)}, u32[]{:S(2)}) %all-to-all-start.1) | async-done | bytes 1048608 | tf_op jit(solution)/shard_map/all_to_all | solution.py:53
  86.7 3.2 %gather_fusion.1 = bf16[128,2048]{1,0:T(8,128)(2,1)} fusion(bf16[16,16,2048]{2,1,0:T(8,128)(2,1)S(1)} %all-to-all-done.1, s32[128]{0:T(128)S(1)} %bitcast.50), kind=kCustom, calls=%fused_computation.1 | custom fusion | bytes 1049600 | tf_op jit(solution)/shard_map/gather | solution.py:87
  90.0 1.5 %fusion.11 = f32[16,2048]{1,0:T(8,128)S(1)} fusion(bf16[128,2048]{1,0:T(8,128)(2,1)} %gather_fusion.1, f32[16,8]{1,0:T(8,128)S(1)} %copy.26), kind=kLoop, calls=%fused_computation.14 | loop fusion | flops 753664 | bytes 655872 | tf_op jit(solution)/shard_map/reduce_sum | solution.py:89
  91.5 0.1 fusion.29
  91.6 2.9 %convolution_convert_fusion.1 = bf16[16,1024]{1,0:T(8,128)(2,1)S(1)} fusion(bf16[2048,1024]{1,0:T(8,128)(2,1)} %param.18, f32[16]{0:T(128)S(1)} %add_rsqrt_fusion, f32[16,2048]{1,0:T(8,128)S(1)} %fusion.11, bf16[16,2048]{1,0:T(8,128)(2,1)S(1)} %copy-done.1), kind=kOutput, calls=%fused_computation.12 | convolution fusion | flops 67321856 | bytes 4423744 | tf_op jit(solution)/shard_map/dot_general | solution.py:19
  94.6 0.7 scatter_custom_fusion.1
  95.3 0.5 broadcast.231
  95.8 0.7 reduce
  96.4 0.6 reshape.208
  97.1 6.9 %all-to-all-start.2 = ((bf16[16,2,512]{2,1,0:T(2,128)(2,1)}), bf16[16,2,512]{2,1,0:T(2,128)(2,1)S(1)}, u32[]{:S(2)}, u32[]{:S(2)}) async-start(bf16[16,2,512]{2,1,0:T(2,128)(2,1)} %reshape.208), calls=%async_computation.2 | async-start | bytes 65536 | tf_op jit(solution)/shard_map/all_to_all | solution.py:100
  104.0 6.5 %all-to-all-done.2 = bf16[16,2,512]{2,1,0:T(2,128)(2,1)S(1)} async-done(((bf16[16,2,512]{2,1,0:T(2,128)(2,1)}), bf16[16,2,512]{2,1,0:T(2,128)(2,1)S(1)}, u32[]{:S(2)}, u32[]{:S(2)}) %all-to-all-start.2) | async-done | bytes 32800 | tf_op jit(solution)/shard_map/all_to_all | solution.py:100
  110.7 1.3 %fusion.23 = bf16[16,4,1024]{2,1,0:T(4,128)(2,1)} fusion(f32[16,4,1024]{2,1,0:T(4,128)S(1)} %broadcast_add_fusion, f32[16,6,1024]{2,1,0:T(8,128)S(1)} %copy-done.2, f32[1024]{0:T(1024)S(1)} %bitcast.61, f32[1024]{0:T(1024)S(1)} %bitcast.62, f32[1024]{0:T(1024)S(1)} %bitcast.57, f32[1024]{0:T(1024)S(1)} %bitcast.58, f32[1024]{0:T(1024)S(1)} %bitcast.59, ...), kind=kLoop, calls=%fused_computation.25 | loop fusion | flops 1179648 | bytes 1734656 | tf_op jit(solution)/shard_map/convert_element_type | solution.py:35
  (35 shorter events, 0.6 us)
Async XLA Ops:
  0.0 54.4 %copy-start = (bf16[1,512,2048]{2,1,0:T(8,128)(2,1)S(1)}, bf16[1,512,2048]{2,1,0:T(8,128)(2,1)}, u32[]{:S(2)}) copy-start(bf16[1,512,2048]{2,1,0:T(8,128)(2,1)} %param.17) | copy-start | bytes 6291460
  0.0 1.6 %copy-start.1 = (bf16[16,2048]{1,0:T(8,128)(2,1)S(1)}, bf16[16,2048]{1,0:T(8,128)(2,1)}, u32[]{:S(2)}) copy-start(bf16[16,2048]{1,0:T(8,128)(2,1)} %param.12) | copy-start | bytes 196612
  20.4 33.2 %copy-start.9 = (bf16[1,2048,512]{2,1,0:T(8,128)(2,1)S(1)}, bf16[1,2048,512]{2,1,0:T(8,128)(2,1)}, u32[]{:S(2)}) copy-start(bf16[1,2048,512]{2,1,0:T(8,128)(2,1)} %param.15) | copy-start | bytes 6291460
  52.6 1.0 copy-start.3
  58.6 5.2 %copy-start.7 = (f32[16,8]{0,1:T(8,128)S(1)}, f32[16,8]{0,1:T(8,128)}, u32[]{:S(2)}) copy-start(f32[16,8]{0,1:T(8,128)} %param.14) | copy-start | bytes 1540
  58.6 5.2 %copy-start.10 = (s32[1,16]{1,0:T(1,128)S(1)}, s32[1,16]{1,0:T(1,128)}, u32[]{:S(2)}) copy-start(s32[1,16]{1,0:T(1,128)} %param.19) | copy-start | bytes 196
  58.6 5.2 %copy-start.5 = (f32[7,1024]{1,0:T(8,128)S(1)}, f32[7,1024]{1,0:T(8,128)}, u32[]{:S(2)}) copy-start(f32[7,1024]{1,0:T(8,128)} %param.23) | copy-start | bytes 86020
  58.6 5.3 %copy-start.4 = (bf16[16,6,1024]{2,0,1:T(8,128)(2,1)S(1)}, bf16[16,6,1024]{2,0,1:T(8,128)(2,1)}, u32[]{:S(2)}) copy-start(bf16[16,6,1024]{2,0,1:T(8,128)(2,1)} %param.21) | copy-start | bytes 589828
  58.7 28.1 %all-to-all-start.1 = ((bf16[16,16,2048]{2,1,0:T(8,128)(2,1)}), bf16[16,16,2048]{2,1,0:T(8,128)(2,1)S(1)}, u32[]{:S(2)}, u32[]{:S(2)}) async-start(bf16[16,16,2048]{2,1,0:T(8,128)(2,1)} %bitcast.51), calls=%async_computation.1 | async-start | bytes 2097152 | tf_op jit(solution)/shard_map/all_to_all | solution.py:53
  91.6 12.4 %copy-start.8 = (s32[16]{0:T(128)S(1)}, s32[16]{0:T(128)}, u32[]{:S(2)}) copy-start(s32[16]{0:T(128)} %param.20) | copy-start | bytes 196
  91.6 19.0 %copy-start.6 = (f32[4,1024]{1,0:T(4,128)S(1)}, f32[4,1024]{1,0:T(4,128)}, u32[]{:S(2)}) copy-start(f32[4,1024]{1,0:T(4,128)} %param.22) | copy-start | bytes 49156
  91.6 19.1 %copy-start.2 = (f32[16,6,1024]{2,1,0:T(8,128)S(1)}, f32[16,6,1024]{2,1,0:T(8,128)}, u32[]{:S(2)}) copy-start(f32[16,6,1024]{2,1,0:T(8,128)} %copy_convert_fusion) | copy-start | bytes 1179652
  97.1 13.5 %all-to-all-start.2 = ((bf16[16,2,512]{2,1,0:T(2,128)(2,1)}), bf16[16,2,512]{2,1,0:T(2,128)(2,1)S(1)}, u32[]{:S(2)}, u32[]{:S(2)}) async-start(bf16[16,2,512]{2,1,0:T(2,128)(2,1)} %reshape.208), calls=%async_computation.2 | async-start | bytes 65536 | tf_op jit(solution)/shard_map/all_to_all | solution.py:100
where the time goes:
time: 113 us; the launch traced here: 112 us
  blocking collectives  32.2 us (28%)
  waiting for transfers between devices  28.4 us (25%)
  local copies, waits for them, and re-layouts  26.2 us (23%)
  starting transfers between devices  12 us (11%)
  matrix products  7.92 us (7%)
  other arithmetic  5.11 us (5%)
    all_to_all x1, blocking collectives, local(): lax.all_to_all(outgoing, 'ep', split_axis=0, concat_axis=0, tiled=True)  32.2 us
    all_to_all x1, waiting for transfers between devices, run_and_return(): lax.all_to_all(outputs, 'ep', split_axis=0, concat_axis=0, tiled=True)  21.9 us
    scatter x1, local copies, waits for them, and re-layouts, local(): outgoing = jnp.zeros((devices, CAP, features), jnp.bfloat16).at[flat_expe...  17 us
    all_to_all x1, starting transfers between devices, local(): lax.all_to_all(placed, 'ep', split_axis=0, concat_axis=0, tiled=True)  6.86 us
    all_to_all x1, waiting for transfers between devices, local(): lax.all_to_all(placed, 'ep', split_axis=0, concat_axis=0, tiled=True)  6.55 us
    all_to_all x1, starting transfers between devices, run_and_return(): lax.all_to_all(outputs, 'ep', split_axis=0, concat_axis=0, tiled=True)  5.14 us
    dot_general x1, matrix products, expert_block(): jnp.dot(inner, down_mat, preferred_element_type=jnp.float32)  4.28 us
    gather x1, local copies, waits for them, and re-layouts, local(): returned[flat_expert, position].astype(jnp.float32)  3.22 us
  transfers between devices with their start and end apart: 2, of which 2 were waited for; matrix products, arithmetic and copies ran while one was open for 1% of the time, Pallas kernels for 0%

commit v1 on v0

--- a/solution.py
+++ b/solution.py
@@ -1,9 +1,14 @@
+import functools
+
 import jax
 import jax.numpy as jnp
 from jax import lax
+from jax.experimental import pallas as pl
+from jax.experimental.pallas import tpu as pltpu
 from jax.sharding import PartitionSpec as P
 
 CAP = 16
+LANES = 128
 
 
 def expert_block(block_rows, gate_mat, up_mat, down_mat):
@@ -51,6 +56,375 @@
         sources, slot_count, features
     )
     return lax.all_to_all(outputs, "ep", split_axis=0, concat_axis=0, tiled=True)
+
+
+def capacity_path(
+    thinker_rows, expert_ids, gate_weights, w_gate, w_up, w_down, talker_proj, talker_slot
+):
+    devices = lax.axis_size("ep")
+    streams_here, features = thinker_rows.shape
+    chosen = expert_ids.shape[1]
+    flat_expert, position = slot_positions(expert_ids, devices)
+    row_index = jnp.arange(streams_here * chosen, dtype=jnp.int32) // chosen
+    outgoing = (
+        jnp.zeros((devices, CAP, features), jnp.bfloat16)
+        .at[flat_expert, position]
+        .set(thinker_rows[row_index])
+    )
+    returned = run_and_return(
+        lax.all_to_all(outgoing, "ep", split_axis=0, concat_axis=0, tiled=True),
+        w_gate,
+        w_up,
+        w_down,
+    )
+    lookup = (
+        returned[flat_expert, position].astype(jnp.float32).reshape(streams_here, chosen, features)
+    )
+    mixture = jnp.sum(gate_weights[:, :, None] * lookup, axis=1)
+    hidden = (thinker_rows.astype(jnp.float32) + mixture).astype(jnp.bfloat16)
+    slots = talker_slot[0]
+    per_owner = streams_here // devices
+    talker_rows = project(hidden, talker_proj)
+    placed = (
+        jnp.zeros_like(talker_rows)
+        .at[slots]
+        .set(talker_rows)
+        .reshape(devices, per_owner, talker_rows.shape[1])
+    )
+    return lax.all_to_all(placed, "ep", split_axis=0, concat_axis=0, tiled=True).reshape(
+        streams_here, talker_rows.shape[1]
+    )
+
+
+def dense_kernel(
+    n,
+    rows_ref,
+    ids_ref,
+    gates_ref,
+    slot_ref,
+    wg_hbm,
+    wu_hbm,
+    wd_hbm,
+    proj_hbm,
+    owned_ref,
+    wg,
+    wu,
+    wd,
+    proj,
+    x_all,
+    inner,
+    part,
+    sib_in,
+    pair_out,
+    y_in,
+    y_out,
+    z_in,
+    row_out,
+    row_in,
+    load_sem,
+    gz_send,
+    gz_recv,
+    gy_send,
+    gy_recv,
+    gs_send,
+    gs_recv,
+    rs_send,
+    rs_recv,
+    ry_send,
+    ry_recv,
+    rz_send,
+    rz_recv,
+    t_send,
+    t_recv,
+):
+    f32, bf16 = jnp.float32, jnp.bfloat16
+    rows, feat = rows_ref.shape
+    hid = wg.shape[1]
+    width = proj.shape[1]
+    line = n // 4
+    half = line * rows
+    tile = min(256, hid)
+    me = lax.axis_index("ep")
+    z = me // 4
+    within = me % 4
+    y = within // 2
+    core = within % 2
+    y_peer = me + 2 - 4 * y
+    sibling = me + 1 - 2 * core
+
+    loads = [
+        pltpu.make_async_copy(src, dst, load_sem.at[i])
+        for i, (src, dst) in enumerate(
+            ((wg_hbm.at[0], wg), (wu_hbm.at[0], wu), (wd_hbm.at[0], wd), (proj_hbm, proj))
+        )
+    ]
+    for load in loads:
+        load.start()
+
+    barrier = pltpu.get_barrier_semaphore()
+    for k in range(1, n):
+        pl.semaphore_signal(barrier, inc=1, device_id={"ep": lax.rem(me + k, n)})
+
+    def block(section, pos):
+        return pl.ds(pl.multiple_of(section * half + pos * rows, rows), rows)
+
+    extra = x_all.shape[1] - feat
+    lane = lax.broadcasted_iota(jnp.int32, (rows, extra), 1)
+    expert_of = lax.rem(lane, n)
+    weight = jnp.zeros((rows, extra), f32)
+    ids = ids_ref[...]
+    gates = gates_ref[...]
+    for j in range(ids.shape[1]):
+        weight = weight + jnp.where(ids[:, j : j + 1] == expert_of, gates[:, j : j + 1], 0.0)
+    high = weight.astype(bf16).astype(f32)
+    mid = (weight - high).astype(bf16).astype(f32)
+    low = weight - high - mid
+    coded = jnp.where(lane < n, high, jnp.where(lane < 2 * n, mid, jnp.where(lane < 3 * n, low, 0.0)))
+    x_all[block(0, z), :feat] = rows_ref[...]
+    x_all[block(0, z), feat:] = coded.astype(bf16)
+
+    pl.semaphore_wait(barrier, n - 1)
+
+    def remote(src, dst, send, recv, peer):
+        return pltpu.make_async_remote_copy(
+            src_ref=src, dst_ref=dst, send_sem=send, recv_sem=recv, device_id={"ep": peer}
+        )
+
+    def z_copy(k):
+        here = x_all.at[block(0, z)]
+        peer = lax.rem(z + k, line) * 4 + within
+        return remote(here, here, gz_send.at[k], gz_recv.at[k], peer)
+
+    def source(k):
+        return lax.rem(z + line - k, line)
+
+    def y_copy(k):
+        return remote(
+            x_all.at[block(0, source(k))],
+            x_all.at[block(1, source(k))],
+            gy_send.at[k],
+            gy_recv.at[k],
+            y_peer,
+        )
+
+    def s_copy(section, k):
+        return remote(
+            x_all.at[block(section, source(k))],
+            x_all.at[block(2 + section, source(k))],
+            gs_send.at[section, k],
+            gs_recv.at[section, k],
+            sibling,
+        )
+
+    gather_z = [z_copy(k) for k in range(1, line)]
+    gather_y = [y_copy(k) for k in range(line)]
+    gather_s = [[s_copy(section, k) for k in range(line)] for section in range(2)]
+    for copy in gather_z:
+        copy.start()
+    gather_y[0].start()
+    gather_s[0][0].start()
+    gather_y[0].wait_recv()
+    gather_s[1][0].start()
+    for k in range(1, line):
+        gather_z[k - 1].wait_recv()
+        gather_y[k].start()
+        gather_s[0][k].start()
+    for k in range(1, line):
+        gather_y[k].wait_recv()
+        gather_s[1][k].start()
+
+    loads[0].wait()
+    loads[1].wait()
+
+    def up_pass(base):
+        span = pl.ds(base, 2 * half)
+
+        def step(j, carry):
+            cols = pl.ds(pl.multiple_of(j * tile, tile), tile)
+            x = x_all[span, :feat]
+            gate_act = jnp.dot(x, wg[:, cols], preferred_element_type=f32)
+            up_act = jnp.dot(x, wu[:, cols], preferred_element_type=f32)
+            inner[span, cols] = (jax.nn.silu(gate_act) * up_act).astype(bf16)
+            return carry
+
+        lax.fori_loop(0, hid // tile, step, 0)
+
+    def down_pass(base):
+        span = pl.ds(base, 2 * half)
+        lanes = lax.broadcasted_iota(jnp.int32, (2 * half, extra), 1)
+        mine = (lax.rem(lanes, n) == me) & (lanes < 3 * n)
+        coef = jnp.sum(
+            jnp.where(mine, x_all[span, feat:].astype(f32), 0.0), axis=1, keepdims=True
+        )
+
+        def step(j, carry):
+            cols = pl.ds(pl.multiple_of(j * tile, tile), tile)
+            out = jnp.dot(inner[span, :], wd[:, cols], preferred_element_type=f32)
+            part[span, cols] = (out * coef).astype(bf16)
+            return carry
+
+        lax.fori_loop(0, feat // tile, step, 0)
+
+    up_pass(0)
+    for section in range(2):
+        for k in range(line):
+            gather_s[section][k].wait_recv()
+    up_pass(2 * half)
+    loads[2].wait()
+    down_pass(2 * half)
+
+    reduce_s = [
+        remote(
+            part.at[pl.ds((2 + section) * half, half)],
+            sib_in.at[pl.ds(section * half, half)],
+            rs_send.at[section],
+            rs_recv.at[section],
+            sibling,
+        )
+        for section in range(2)
+    ]
+    reduce_s[1].start()
+    reduce_s[0].start()
+    down_pass(0)
+
+    def target(k):
+        return lax.rem(z + k, line)
+
+    reduce_y = [
+        remote(
+            pair_out.at[block(0, target(k))],
+            y_in.at[block(0, target(k))],
+            ry_send.at[k],
+            ry_recv.at[k],
+            y_peer,
+        )
+        for k in range(line)
+    ]
+    reduce_z = [
+        remote(
+            y_out.at[block(0, target(k))],
+            z_in.at[block(0, k)],
+            rz_send.at[k],
+            rz_recv.at[k],
+            target(k) * 4 + within,
+        )
+        for k in range(1, line)
+    ]
+    order = list(range(1, line)) + [0]
+    reduce_s[1].wait_recv()
+    for k in order:
+        far = block(1, target(k))
+        pair_out[block(0, target(k)), :] = (
+            part[far, :].astype(f32) + sib_in[far, :].astype(f32)
+        ).astype(bf16)
+        reduce_y[k].start()
+    reduce_s[0].wait_recv()
+    for k in range(1, line):
+        here = block(0, target(k))
+        reduce_y[k].wait_recv()
+        y_out[here, :] = (
+            part[here, :].astype(f32) + sib_in[here, :].astype(f32) + y_in[here, :].astype(f32)
+        ).astype(bf16)
+        reduce_z[k - 1].start()
+    here = block(0, z)
+    reduce_y[0].wait_recv()
+    total = (
+        rows_ref[...].astype(f32)
+        + part[here, :].astype(f32)
+        + sib_in[here, :].astype(f32)
+        + y_in[here, :].astype(f32)
+    )
+    for k in range(1, line):
+        reduce_z[k - 1].wait_recv()
+        total = total + z_in[k * rows : (k + 1) * rows, :].astype(f32)
+    hidden = total.astype(bf16).astype(f32)
+    scale = lax.rsqrt(jnp.mean(hidden * hidden, axis=-1, keepdims=True) + 1e-06)
+    normed = (hidden * scale).astype(bf16)
+
+    owner = lax.broadcasted_iota(jnp.int32, (n, rows), 0)
+    pick = jnp.where(owner == slot_ref[...], 1.0, 0.0).astype(bf16)
+    loads[3].wait()
+    for j in range(width // tile):
+        talk = jnp.dot(
+            normed, proj[:, j * tile : (j + 1) * tile], preferred_element_type=f32
+        ).astype(bf16)
+        ordered = jnp.dot(pick, talk, preferred_element_type=f32)
+        for i in range(tile // LANES):
+            row_out[:, j * (tile // LANES) + i, :] = ordered[:, i * LANES : (i + 1) * LANES]
+    exchange = []
+    for k in range(1, n):
+        peer = lax.rem(me + k, n)
+        exchange.append(
+            remote(row_out.at[peer], row_in.at[me], t_send.at[k], t_recv.at[k], peer)
+        )
+    for copy in exchange:
+        copy.start()
+    row_in[pl.ds(me, 1)] = row_out[pl.ds(me, 1)]
+    for copy in exchange:
+        copy.wait_recv()
+    for i in range(width // LANES):
+        owned_ref[:, i * LANES : (i + 1) * LANES] = row_in[:, i, :]
+
+    for copy in (
+        gather_z + gather_y + gather_s[0] + gather_s[1] + reduce_s + reduce_y + reduce_z + exchange
+    ):
+        copy.wait_send()
+
+
+def dense_path(
+    thinker_rows, expert_ids, gate_weights, w_gate, w_up, w_down, talker_proj, talker_slot
+):
+    n = lax.axis_size("ep")
+    rows, feat = thinker_rows.shape
+    hid = w_gate.shape[2]
+    width = talker_proj.shape[1]
+    line = n // 4
+    every = n * rows
+    extra = -(-3 * n // LANES) * LANES
+    bf16, f32 = jnp.bfloat16, jnp.float32
+    vmem = pl.BlockSpec(memory_space=pltpu.VMEM)
+    hbm = pl.BlockSpec(memory_space=pl.ANY)
+    dma = pltpu.SemaphoreType.DMA
+    return pl.pallas_call(
+        functools.partial(dense_kernel, n),
+        out_shape=jax.ShapeDtypeStruct((rows, width), f32),
+        in_specs=[vmem] * 4 + [hbm] * 4,
+        out_specs=vmem,
+        scratch_shapes=[
+            pltpu.VMEM((feat, hid), bf16),
+            pltpu.VMEM((feat, hid), bf16),
+            pltpu.VMEM((hid, feat), bf16),
+            pltpu.VMEM((feat, width), bf16),
+            pltpu.VMEM((every, feat + extra), bf16),
+            pltpu.VMEM((every, hid), bf16),
+            pltpu.VMEM((every, feat), bf16),
+            pltpu.VMEM((every // 2, feat), bf16),
+            pltpu.VMEM((line * rows, feat), bf16),
+            pltpu.VMEM((line * rows, feat), bf16),
+            pltpu.VMEM((line * rows, feat), bf16),
+            pltpu.VMEM((line * rows, feat), bf16),
+            pltpu.VMEM((n, width // LANES, LANES), f32),
+            pltpu.VMEM((n, width // LANES, LANES), f32),
+            dma((4,)),
+            dma((line,)),
+            dma((line,)),
+            dma((line,)),
+            dma((line,)),
+            dma((2, line)),
+            dma((2, line)),
+            dma((2,)),
+            dma((2,)),
+            dma((line,)),
+            dma((line,)),
+            dma((line,)),
+            dma((line,)),
+            dma((n,)),
+            dma((n,)),
+        ],
+        compiler_params=pltpu.CompilerParams(
+            collective_id=0, has_side_effects=True, vmem_limit_bytes=48 * 1024 * 1024
+        ),
+    )(thinker_rows, expert_ids, gate_weights, talker_slot, w_gate, w_up, w_down, talker_proj)
 
 
 def local(
@@ -68,37 +442,11 @@
     conv_weight,
 ):
     devices = lax.axis_size("ep")
-    streams_here, features = thinker_rows.shape
-    chosen = expert_ids.shape[1]
-    flat_expert, position = slot_positions(expert_ids, devices)
-    row_index = jnp.arange(streams_here * chosen, dtype=jnp.int32) // chosen
-    outgoing = (
-        jnp.zeros((devices, CAP, features), jnp.bfloat16)
-        .at[flat_expert, position]
-        .set(thinker_rows[row_index])
-    )
-    returned = run_and_return(
-        lax.all_to_all(outgoing, "ep", split_axis=0, concat_axis=0, tiled=True),
-        w_gate,
-        w_up,
-        w_down,
-    )
-    lookup = (
-        returned[flat_expert, position].astype(jnp.float32).reshape(streams_here, chosen, features)
-    )
-    mixture = jnp.sum(gate_weights[:, :, None] * lookup, axis=1)
-    hidden = (thinker_rows.astype(jnp.float32) + mixture).astype(jnp.bfloat16)
-    slots = talker_slot[0]
-    per_owner = streams_here // devices
-    talker_rows = project(hidden, talker_proj)
-    placed = (
-        jnp.zeros_like(talker_rows)
-        .at[slots]
-        .set(talker_rows)
-        .reshape(devices, per_owner, talker_rows.shape[1])
-    )
-    owned = lax.all_to_all(placed, "ep", split_axis=0, concat_axis=0, tiled=True).reshape(
-        streams_here, talker_rows.shape[1]
+    streams_here = thinker_rows.shape[0]
+    dense = streams_here <= CAP and streams_here == devices and devices % 4 == 0
+    path = dense_path if dense else capacity_path
+    owned = path(
+        thinker_rows, expert_ids, gate_weights, w_gate, w_up, w_down, talker_proj, talker_slot
     )
     return vocode(owned, speech_count, left_context, frame_offset, conv_weight)
 

time: 113 us -> 49.9 us (0.44)
  Pallas kernels: 0 us -> 40.1 us
  blocking collectives: 32.2 us -> 0 us
  waiting for transfers between devices: 28.4 us -> 0 us
  local copies, waits for them, and re-layouts: 26.2 us -> 7.24 us
  starting transfers between devices: 12 us -> 0 us
  matrix products: 7.92 us -> 0 us
  other arithmetic: 5.11 us -> 2.2 us
    pallas_call x0 -> x1, Pallas kernels: none -> 40.1 us  [dense_path(): pl.pallas_call(functools.partial(dense_kernel, n), out_shape=jax.ShapeDty...]
    all_to_all x1 -> x0, blocking collectives: 32.2 us -> none  [local(): lax.all_to_all(outgoing, 'ep', split_axis=0, concat_axis=0, tiled=True)]
    all_to_all x2 -> x0, waiting for transfers between devices: 28.4 us -> none  [the longest x1 21.9 us: run_and_return(): lax.all_to_all(outputs, 'ep', split_axis=0, concat_axis=0, tiled=True)]
    scatter x2 -> x0, local copies, waits for them, and re-layouts: 17.7 us -> none  [the longest x1 17 us: local(): outgoing = jnp.zeros((devices, CAP, features), jnp.bfloat16).at[flat_expe...]
    all_to_all x2 -> x0, starting transfers between devices: 12 us -> none  [the longest x1 6.86 us: local(): lax.all_to_all(placed, 'ep', split_axis=0, concat_axis=0, tiled=True)]
    dot_general x3 -> x0, matrix products: 7.92 us -> none  [the longest x1 4.28 us: expert_block(): jnp.dot(inner, down_mat, preferred_element_type=jnp.float32)]
    gather x2 -> x0, local copies, waits for them, and re-layouts: 4.94 us -> none  [the longest x1 3.22 us: local(): returned[flat_expert, position].astype(jnp.float32)]
    unnamed x27 -> x14, local copies, waits for them, and re-layouts: 2.74 us -> 6.19 us
  transfers between devices with their start and end apart: 2 -> 0, of which waited for: 2 -> 0; matrix products, arithmetic and copies ran while one was open for 1% -> 0% of each run, Pallas kernels for 0% -> 0%
where the time goes in v1:
time: 49.9 us; the launch traced here: 49.6 us
  Pallas kernels  40.1 us (80%)
  local copies, waits for them, and re-layouts  7.24 us (15%)
  other arithmetic  2.2 us (4%)
    pallas_call x1, Pallas kernels, dense_path(): pl.pallas_call(functools.partial(dense_kernel, n), out_shape=jax.ShapeDty...  40.1 us
    unnamed x14, local copies, waits for them, and re-layouts  6.19 us
    convert_element_type x1, other arithmetic, vocode(): return jnp.where(active, result, 0.0).astype(jnp.bfloat16)  1.29 us
    slice x1, local copies, waits for them, and re-layouts, vocode(): conv_weight[offset][None, None, :] * sequence[:, offset:offset + horizon, :]  1.04 us

profile of v1, /device:TPU:0, one launch (start us, length us, event | category | flops | bytes accessed | tf_op | source)
XLA Modules:
  0.0 49.6 jit_solution(6672259918994925318)
XLA Ops:
  0.0 0.7 %iota_compare_fusion = pred[16,4]{1,0:T(8,128)(4,1)S(1)} fusion(s32[16]{0:T(128)} %param.20), kind=kLoop, calls=%fused_computation.17 | loop fusion | flops 64 | bytes 128 | tf_op jit(solution)/shard_map/lt | solution.py:39
  0.7 0.8 %copy.14.ids_ref = s32[16,8]{1,0:T(8,128)S(1)} copy(s32[16,8]{0,1:T(8,128)} %param.13) | data formatting | bytes 1024 | tf_op args[1]
  1.5 0.8 %copy.15.gates_ref = f32[16,8]{1,0:T(8,128)S(1)} copy(f32[16,8]{0,1:T(8,128)} %param.14) | data formatting | bytes 1024 | tf_op args[2]
  2.2 1.0 %fusion.9 = (f32[1,1024]{1,0:T(1,128)S(1)}, f32[1,1024]{1,0:T(1,128)S(1)}, f32[1,1024]{1,0:T(1,128)S(1)}, f32[1,1024]{1,0:T(1,128)S(1)}, f32[1,1024]{1,0:T(1,128...) fusion(f32[7,1024]{1,0:T(8,128)} %param.23), kind=kLoop, calls=%fused_computation.18 | loop fusion | bytes 57344 | tf_op jit(solution)/shard_map/slice | solution.py:37
  3.3 0.0 copy-start
  3.3 1.6 %copy-done = bf16[1,2048,512]{2,1,0:T(8,128)(2,1)S(1)} copy-done((bf16[1,2048,512]{2,1,0:T(8,128)(2,1)S(1)}, bf16[1,2048,512]{2,1,0:T(8,128)(2,1)}, u32[]{:S(2)}) %copy-start) | copy-done | bytes 2097176
  4.9 0.0 copy-start.1
  4.9 1.6 %copy-done.1 = bf16[1,2048,512]{2,1,0:T(8,128)(2,1)S(1)} copy-done((bf16[1,2048,512]{2,1,0:T(8,128)(2,1)S(1)}, bf16[1,2048,512]{2,1,0:T(8,128)(2,1)}, u32[]{:S(2)}) %copy-start.1) | copy-done | bytes 2097176
  6.5 0.0 copy-start.2
  6.5 0.8 %copy-done.2 = bf16[16,2048]{1,0:T(8,128)(2,1)S(1)} copy-done((bf16[16,2048]{1,0:T(8,128)(2,1)S(1)}, bf16[16,2048]{1,0:T(8,128)(2,1)}, u32[]{:S(2)}) %copy-start.2) | copy-done | bytes 65560
  7.3 0.0 copy-start.3
  7.3 0.7 %copy-done.3 = s32[1,16]{1,0:T(1,128)S(1)} copy-done((s32[1,16]{1,0:T(1,128)S(1)}, s32[1,16]{1,0:T(1,128)}, u32[]{:S(2)}) %copy-start.3) | copy-done | bytes 88
  8.0 0.0 copy-start.5
  8.0 0.0 copy-start.4
  8.0 40.1 %shard_map.118 = f32[16,1024]{1,0:T(8,128)S(1)} custom-call(bf16[16,2048]{1,0:T(8,128)(2,1)S(1)} %copy-done.2, s32[16,8]{1,0:T(8,128)S(1)} %copy.14.ids_ref, f32[16,8]{1,0:T(8,128)S(1)} %copy.15.gates_ref, s32[1,16]{1,0:T(1,128)S(1)} %copy-done.3, bf16[1,2048,512]{2,1,0:T(8,128)(2,1)S(1)} %copy-done, bf16[1,2048,512]{2,1,0:T(8,128)(2,1)S(1)} %copy-done.1, ...), custom_call_target="tpu_custom_call" | custom-call | tf_op jit(solution)/shard_map/pallas_call | solution.py:388
  48.0 0.0 copy-done.5
  48.1 0.1 broadcast_add_fusion
  48.1 0.0 copy-done.4
  48.1 0.1 copy_convert_fusion
  48.3 1.3 %fusion.4 = bf16[16,4,1024]{2,1,0:T(4,128)(2,1)} fusion(f32[16,4,1024]{2,1,0:T(4,128)S(1)} %broadcast_add_fusion, f32[16,6,1024]{2,1,0:T(8,128)S(1)} %copy_convert_fusion, f32[1024]{0:T(1024)S(1)} %bitcast.12, f32[1024]{0:T(1024)S(1)} %bitcast.13, f32[1024]{0:T(1024)S(1)} %bitcast.8, f32[1024]{0:T(1024)S(1)} %bitcast.9, f32[1024]{0:T(1024)S(1)} %bitcast.10, ...), kind=kLoop, calls=%fused_computation.5 | loop fusion | flops 1179648 | bytes 1734656 | tf_op jit(solution)/shard_map/convert_element_type | solution.py:40
Async XLA Ops:
  3.3 1.6 %copy-start = (bf16[1,2048,512]{2,1,0:T(8,128)(2,1)S(1)}, bf16[1,2048,512]{2,1,0:T(8,128)(2,1)}, u32[]{:S(2)}) copy-start(bf16[1,2048,512]{2,1,0:T(8,128)(2,1)} %wg_hbm.1) | copy-start | bytes 6291460
  4.9 1.6 %copy-start.1 = (bf16[1,2048,512]{2,1,0:T(8,128)(2,1)S(1)}, bf16[1,2048,512]{2,1,0:T(8,128)(2,1)}, u32[]{:S(2)}) copy-start(bf16[1,2048,512]{2,1,0:T(8,128)(2,1)} %wu_hbm.1) | copy-start | bytes 6291460
  6.5 0.8 %copy-start.2 = (bf16[16,2048]{1,0:T(8,128)(2,1)S(1)}, bf16[16,2048]{1,0:T(8,128)(2,1)}, u32[]{:S(2)}) copy-start(bf16[16,2048]{1,0:T(8,128)(2,1)} %rows_ref.1) | copy-start | bytes 196612
  7.3 0.7 %copy-start.3 = (s32[1,16]{1,0:T(1,128)S(1)}, s32[1,16]{1,0:T(1,128)}, u32[]{:S(2)}) copy-start(s32[1,16]{1,0:T(1,128)} %slot_ref.1) | copy-start | bytes 196
  8.0 40.1 %copy-start.5 = (f32[4,1024]{1,0:T(4,128)S(1)}, f32[4,1024]{1,0:T(4,128)}, u32[]{:S(2)}) copy-start(f32[4,1024]{1,0:T(4,128)} %param.22) | copy-start | bytes 49156
  8.0 40.2 %copy-start.4 = (bf16[16,6,1024]{2,0,1:T(8,128)(2,1)S(1)}, bf16[16,6,1024]{2,0,1:T(8,128)(2,1)}, u32[]{:S(2)}) copy-start(bf16[16,6,1024]{2,0,1:T(8,128)(2,1)} %param.21) | copy-start | bytes 589828

commit v2 on v1

--- a/solution.py
+++ b/solution.py
@@ -98,15 +98,27 @@
 
 def dense_kernel(
     n,
-    rows_ref,
-    ids_ref,
-    gates_ref,
-    slot_ref,
+    rows_hbm,
+    ids_hbm,
+    gates_hbm,
+    slot_hbm,
+    count_hbm,
+    context_hbm,
+    offset_hbm,
+    taps_hbm,
     wg_hbm,
     wu_hbm,
     wd_hbm,
     proj_hbm,
-    owned_ref,
+    voice_ref,
+    ids_ref,
+    gates_ref,
+    slot_ref,
+    count_ref,
+    context,
+    frame_offset,
+    taps,
+    base_voice,
     wg,
     wu,
     wd,
@@ -138,7 +150,7 @@
     t_recv,
 ):
     f32, bf16 = jnp.float32, jnp.bfloat16
-    rows, feat = rows_ref.shape
+    rows, feat = rows_hbm.shape
     hid = wg.shape[1]
     width = proj.shape[1]
     line = n // 4
@@ -152,10 +164,27 @@
     y_peer = me + 2 - 4 * y
     sibling = me + 1 - 2 * core
 
+    def block(section, pos):
+        return pl.ds(pl.multiple_of(section * half + pos * rows, rows), rows)
+
+    own = block(0, z)
     loads = [
         pltpu.make_async_copy(src, dst, load_sem.at[i])
         for i, (src, dst) in enumerate(
-            ((wg_hbm.at[0], wg), (wu_hbm.at[0], wu), (wd_hbm.at[0], wd), (proj_hbm, proj))
+            (
+                (rows_hbm, x_all.at[own, pl.ds(0, feat)]),
+                (ids_hbm, ids_ref),
+                (gates_hbm, gates_ref),
+                (slot_hbm, slot_ref),
+                (count_hbm, count_ref),
+                (context_hbm, context),
+                (offset_hbm, frame_offset),
+                (taps_hbm, taps),
+                (wg_hbm.at[0], wg),
+                (wu_hbm.at[0], wu),
+                (wd_hbm.at[0], wd),
+                (proj_hbm, proj),
+            )
         )
     ]
     for load in loads:
@@ -165,23 +194,29 @@
     for k in range(1, n):
         pl.semaphore_signal(barrier, inc=1, device_id={"ep": lax.rem(me + k, n)})
 
-    def block(section, pos):
-        return pl.ds(pl.multiple_of(section * half + pos * rows, rows), rows)
-
     extra = x_all.shape[1] - feat
-    lane = lax.broadcasted_iota(jnp.int32, (rows, extra), 1)
-    expert_of = lax.rem(lane, n)
-    weight = jnp.zeros((rows, extra), f32)
-    ids = ids_ref[...]
-    gates = gates_ref[...]
-    for j in range(ids.shape[1]):
-        weight = weight + jnp.where(ids[:, j : j + 1] == expert_of, gates[:, j : j + 1], 0.0)
+    spot = lax.broadcasted_iota(jnp.int32, (extra, rows), 0)
+    expert_of = lax.rem(spot, n)
+    weight = jnp.zeros((extra, rows), f32)
+    for load in loads[:5]:
+        load.wait()
+    for j in range(ids_ref.shape[0]):
+        weight = weight + jnp.where(
+            ids_ref[j : j + 1, :] == expert_of, gates_ref[j : j + 1, :], 0.0
+        )
     high = weight.astype(bf16).astype(f32)
     mid = (weight - high).astype(bf16).astype(f32)
     low = weight - high - mid
-    coded = jnp.where(lane < n, high, jnp.where(lane < 2 * n, mid, jnp.where(lane < 3 * n, low, 0.0)))
-    x_all[block(0, z), :feat] = rows_ref[...]
-    x_all[block(0, z), feat:] = coded.astype(bf16)
+    coded = jnp.where(spot < n, high, jnp.where(spot < 2 * n, mid, jnp.where(spot < 3 * n, low, 0.0)))
+    diagonal = lax.broadcasted_iota(jnp.int32, (rows, rows), 0) == lax.broadcasted_iota(
+        jnp.int32, (rows, rows), 1
+    )
+    x_all[own, feat:] = lax.dot_general(
+        jnp.where(diagonal, 1.0, 0.0).astype(bf16),
+        coded.astype(bf16),
+        (((1,), (1,)), ((), ())),
+        preferred_element_type=f32,
+    ).astype(bf16)
 
     pl.semaphore_wait(barrier, n - 1)
 
@@ -223,6 +258,21 @@
         copy.start()
     gather_y[0].start()
     gather_s[0][0].start()
+
+    for load in loads[5:8]:
+        load.wait()
+    before = context.shape[0]
+    horizon = frame_offset.shape[0]
+    for f in range(horizon):
+        voice = jnp.zeros((rows, width), f32)
+        for t in range(taps.shape[0]):
+            tap = taps[t : t + 1, :]
+            if f + t < before:
+                voice = voice + tap * context[f + t].astype(f32)
+            else:
+                voice = voice + tap * frame_offset[f + t - before : f + t - before + 1, :]
+        base_voice[f] = voice
+
     gather_y[0].wait_recv()
     gather_s[1][0].start()
     for k in range(1, line):
@@ -233,8 +283,8 @@
         gather_y[k].wait_recv()
         gather_s[1][k].start()
 
-    loads[0].wait()
-    loads[1].wait()
+    loads[8].wait()
+    loads[9].wait()
 
     def up_pass(base):
         span = pl.ds(base, 2 * half)
@@ -270,7 +320,7 @@
         for k in range(line):
             gather_s[section][k].wait_recv()
     up_pass(2 * half)
-    loads[2].wait()
+    loads[10].wait()
     down_pass(2 * half)
 
     reduce_s = [
@@ -329,7 +379,7 @@
     here = block(0, z)
     reduce_y[0].wait_recv()
     total = (
-        rows_ref[...].astype(f32)
+        x_all[own, :feat].astype(f32)
         + part[here, :].astype(f32)
         + sib_in[here, :].astype(f32)
         + y_in[here, :].astype(f32)
@@ -343,7 +393,7 @@
 
     owner = lax.broadcasted_iota(jnp.int32, (n, rows), 0)
     pick = jnp.where(owner == slot_ref[...], 1.0, 0.0).astype(bf16)
-    loads[3].wait()
+    loads[11].wait()
     for j in range(width // tile):
         talk = jnp.dot(
             normed, proj[:, j * tile : (j + 1) * tile], preferred_element_type=f32
@@ -362,8 +412,16 @@
     row_in[pl.ds(me, 1)] = row_out[pl.ds(me, 1)]
     for copy in exchange:
         copy.wait_recv()
+    count = jnp.sum(
+        jnp.where(diagonal, count_ref[...].astype(f32), 0.0), axis=1, keepdims=True
+    )
     for i in range(width // LANES):
-        owned_ref[:, i * LANES : (i + 1) * LANES] = row_in[:, i, :]
+        cols = slice(i * LANES, (i + 1) * LANES)
+        owned = row_in[:, i, :]
+        for f in range(horizon):
+            gain = jnp.sum(taps[before - f :, cols], axis=0, keepdims=True)
+            voice = base_voice[f, :, cols] + gain * owned
+            voice_ref[f, :, cols] = jnp.where(count > f, voice, 0.0).astype(bf16)
 
     for copy in (
         gather_z + gather_y + gather_s[0] + gather_s[1] + reduce_s + reduce_y + reduce_z + exchange
@@ -372,7 +430,18 @@
 
 
 def dense_path(
-    thinker_rows, expert_ids, gate_weights, w_gate, w_up, w_down, talker_proj, talker_slot
+    thinker_rows,
+    expert_ids,
+    gate_weights,
+    w_gate,
+    w_up,
+    w_down,
+    talker_proj,
+    talker_slot,
+    speech_count,
+    left_context,
+    frame_offset,
+    conv_weight,
 ):
     n = lax.axis_size("ep")
     rows, feat = thinker_rows.shape
@@ -382,15 +451,26 @@
     every = n * rows
     extra = -(-3 * n // LANES) * LANES
     bf16, f32 = jnp.bfloat16, jnp.float32
+    chosen = expert_ids.shape[1]
+    before = left_context.shape[1]
+    horizon = frame_offset.shape[0]
     vmem = pl.BlockSpec(memory_space=pltpu.VMEM)
     hbm = pl.BlockSpec(memory_space=pl.ANY)
     dma = pltpu.SemaphoreType.DMA
-    return pl.pallas_call(
+    voice = pl.pallas_call(
         functools.partial(dense_kernel, n),
-        out_shape=jax.ShapeDtypeStruct((rows, width), f32),
-        in_specs=[vmem] * 4 + [hbm] * 4,
+        out_shape=jax.ShapeDtypeStruct((horizon, rows, width), bf16),
+        in_specs=[hbm] * 12,
         out_specs=vmem,
         scratch_shapes=[
+            pltpu.VMEM((chosen, rows), jnp.int32),
+            pltpu.VMEM((chosen, rows), f32),
+            pltpu.VMEM((1, rows), jnp.int32),
+            pltpu.VMEM((1, rows), jnp.int32),
+            pltpu.VMEM((before, rows, width), bf16),
+            pltpu.VMEM((horizon, width), f32),
+            pltpu.VMEM(conv_weight.shape, f32),
+            pltpu.VMEM((horizon, rows, width), f32),
             pltpu.VMEM((feat, hid), bf16),
             pltpu.VMEM((feat, hid), bf16),
             pltpu.VMEM((hid, feat), bf16),
@@ -405,7 +485,7 @@
             pltpu.VMEM((line * rows, feat), bf16),
             pltpu.VMEM((n, width // LANES, LANES), f32),
             pltpu.VMEM((n, width // LANES, LANES), f32),
-            dma((4,)),
+            dma((12,)),
             dma((line,)),
             dma((line,)),
             dma((line,)),
@@ -422,9 +502,23 @@
             dma((n,)),
         ],
         compiler_params=pltpu.CompilerParams(
-            collective_id=0, has_side_effects=True, vmem_limit_bytes=48 * 1024 * 1024
+            collective_id=0, has_side_effects=True, vmem_limit_bytes=60 * 1024 * 1024
         ),
-    )(thinker_rows, expert_ids, gate_weights, talker_slot, w_gate, w_up, w_down, talker_proj)
+    )(
+        thinker_rows,
+        expert_ids.T,
+        gate_weights.T,
+        talker_slot,
+        speech_count.reshape(1, rows),
+        left_context.transpose(1, 0, 2),
+        frame_offset,
+        conv_weight,
+        w_gate,
+        w_up,
+        w_down,
+        talker_proj,
+    )
+    return voice.transpose(1, 0, 2)
 
 
 def local(
@@ -444,11 +538,13 @@
     devices = lax.axis_size("ep")
     streams_here = thinker_rows.shape[0]
     dense = streams_here <= CAP and streams_here == devices and devices % 4 == 0
-    path = dense_path if dense else capacity_path
-    owned = path(
+    experts = (
         thinker_rows, expert_ids, gate_weights, w_gate, w_up, w_down, talker_proj, talker_slot
     )
-    return vocode(owned, speech_count, left_context, frame_offset, conv_weight)
+    voices = (speech_count, left_context, frame_offset, conv_weight)
+    if dense:
+        return dense_path(*experts, *voices)
+    return vocode(capacity_path(*experts), *voices)
 
 
 def solution(mesh):

time: 49.9 us -> 42.4 us (0.85)
  local copies, waits for them, and re-layouts: 7.24 us -> 1.66 us
  other arithmetic: 2.2 us -> 0 us
    unnamed x14 -> x0, local copies, waits for them, and re-layouts: 6.19 us -> none
    transpose x0 -> x1, local copies, waits for them, and re-layouts: none -> 1.66 us  [dense_path(): return voice.transpose(1, 0, 2)]
    convert_element_type x2 -> x0, other arithmetic: 1.41 us -> none  [the longest x1 1.29 us: vocode(): return jnp.where(active, result, 0.0).astype(jnp.bfloat16)]
    slice x1 -> x0, local copies, waits for them, and re-layouts: 1.04 us -> none  [vocode(): conv_weight[offset][None, None, :] * sequence[:, offset:offset + horizon, :]]
    lt x1 -> x0, other arithmetic: 0.73 us -> none  [vocode(): jnp.arange(horizon, dtype=jnp.int32)[None, :, None]]
where the time goes in v2:
time: 42.4 us; the launch traced here: 42.2 us
  Pallas kernels  40.5 us (96%)
  local copies, waits for them, and re-layouts  1.66 us (4%)
    pallas_call x1, Pallas kernels, dense_path(): pl.pallas_call(functools.partial(dense_kernel, n), out_shape=jax.ShapeDty...  40.5 us
    transpose x1, local copies, waits for them, and re-layouts, dense_path(): return voice.transpose(1, 0, 2)  1.66 us

profile of v2, /device:TPU:0, one launch (start us, length us, event | category | flops | bytes accessed | tf_op | source)
XLA Modules:
  0.0 42.2 jit_solution(10354431501839195193)
XLA Ops:
  0.0 40.5 %shard_map.118 = bf16[4,16,1024]{2,1,0:T(8,128)(2,1)} custom-call(bf16[16,2048]{1,0:T(8,128)(2,1)} %rows_hbm.1, s32[8,16]{1,0:T(8,128)} %bitcast.7, f32[8,16]{1,0:T(8,128)} %bitcast.8, s32[1,16]{1,0:T(1,128)} %slot_hbm.1, s32[1,16]{1,0:T(1,128)} %bitcast.9, bf16[6,16,1024]{2,1,0:T(8,128)(2,1)} %bitcast.6, f32[4,1024]{1,0:T(4,128)} %offset_hbm.1, ...), custom_call_target="tpu_custom_call" | custom-call | tf_op jit(solution)/shard_map/pallas_call | solution.py:460
  40.5 1.7 %copy.13 = bf16[16,4,1024]{2,1,0:T(4,128)(2,1)} copy(bf16[16,4,1024]{2,0,1:T(8,128)(2,1)} %bitcast.5) | data formatting | bytes 262144 | tf_op jit(solution)/shard_map/transpose | solution.py:521

commit v3 on v2

--- a/solution.py
+++ b/solution.py
@@ -225,39 +225,57 @@
             src_ref=src, dst_ref=dst, send_sem=send, recv_sem=recv, device_id={"ep": peer}
         )
 
-    def z_copy(k):
-        here = x_all.at[block(0, z)]
-        peer = lax.rem(z + k, line) * 4 + within
-        return remote(here, here, gz_send.at[k], gz_recv.at[k], peer)
-
-    def source(k):
-        return lax.rem(z + line - k, line)
-
-    def y_copy(k):
+    def z_copy(up, src):
+        here = x_all.at[block(0, src)]
+        step = 4 if up else -4
+        return remote(here, here, gz_send.at[int(up), src], gz_recv.at[src], me + step)
+
+    def y_copy(src):
         return remote(
-            x_all.at[block(0, source(k))],
-            x_all.at[block(1, source(k))],
-            gy_send.at[k],
-            gy_recv.at[k],
+            x_all.at[block(0, src)],
+            x_all.at[block(2, src)],
+            gy_send.at[src],
+            gy_recv.at[src],
             y_peer,
         )
 
-    def s_copy(section, k):
+    def s_copy(section, src):
         return remote(
-            x_all.at[block(section, source(k))],
-            x_all.at[block(2 + section, source(k))],
-            gs_send.at[section, k],
-            gs_recv.at[section, k],
+            x_all.at[block(2 * section, src)],
+            x_all.at[block(2 * section + 1, src)],
+            gs_send.at[section, src],
+            gs_recv.at[section, src],
             sibling,
         )
 
-    gather_z = [z_copy(k) for k in range(1, line)]
-    gather_y = [y_copy(k) for k in range(line)]
-    gather_s = [[s_copy(section, k) for k in range(line)] for section in range(2)]
-    for copy in gather_z:
-        copy.start()
-    gather_y[0].start()
-    gather_s[0][0].start()
+    def at_distance(d, use):
+        for src in (z,) if d == 0 else (z - d, z + d):
+            pl.when((src >= 0) & (src < line))(functools.partial(use, src))
+
+    def pass_z(d, act):
+        def go(up, src):
+            pl.when((z + 1 < line) if up else (z > 0))(lambda: act(z_copy(up, src)))
+
+        if d == 0:
+            go(True, z)
+            go(False, z)
+        else:
+            pl.when(z - d >= 0)(lambda: go(True, z - d))
+            pl.when(z + d < line)(lambda: go(False, z + d))
+
+    def from_z(d):
+        at_distance(d, lambda src: z_copy(True, src).wait_recv())
+
+    def hand_on(src):
+        y_copy(src).start()
+        s_copy(0, src).start()
+
+    def from_y(src):
+        y_copy(src).wait_recv()
+        s_copy(1, src).start()
+
+    pass_z(0, lambda copy: copy.start())
+    hand_on(z)
 
     for load in loads[5:8]:
         load.wait()
@@ -273,15 +291,12 @@
                 voice = voice + tap * frame_offset[f + t - before : f + t - before + 1, :]
         base_voice[f] = voice
 
-    gather_y[0].wait_recv()
-    gather_s[1][0].start()
-    for k in range(1, line):
-        gather_z[k - 1].wait_recv()
-        gather_y[k].start()
-        gather_s[0][k].start()
-    for k in range(1, line):
-        gather_y[k].wait_recv()
-        gather_s[1][k].start()
+    for d in range(1, line):
+        from_z(d)
+        pass_z(d, lambda copy: copy.start())
+        at_distance(d, hand_on)
+        if d < line - 1:
+            at_distance(d - 1, from_y)
 
     loads[8].wait()
     loads[9].wait()
@@ -299,7 +314,7 @@
 
         lax.fori_loop(0, hid // tile, step, 0)
 
-    def down_pass(base):
+    def down_pass(base, cut):
         span = pl.ds(base, 2 * half)
         lanes = lax.broadcasted_iota(jnp.int32, (2 * half, extra), 1)
         mine = (lax.rem(lanes, n) == me) & (lanes < 3 * n)
@@ -308,84 +323,115 @@
         )
 
         def step(j, carry):
-            cols = pl.ds(pl.multiple_of(j * tile, tile), tile)
+            cols = pl.ds(pl.multiple_of(cut * piece + j * tile, tile), tile)
             out = jnp.dot(inner[span, :], wd[:, cols], preferred_element_type=f32)
             part[span, cols] = (out * coef).astype(bf16)
             return carry
 
-        lax.fori_loop(0, feat // tile, step, 0)
-
-    up_pass(0)
-    for section in range(2):
-        for k in range(line):
-            gather_s[section][k].wait_recv()
-    up_pass(2 * half)
-    loads[10].wait()
-    down_pass(2 * half)
+        lax.fori_loop(0, piece // tile, step, 0)
+
+    cuts = rs_send.shape[1]
+    piece = feat // cuts
+
+    def columns(cut):
+        return pl.ds(cut * piece, piece)
 
     reduce_s = [
-        remote(
-            part.at[pl.ds((2 + section) * half, half)],
-            sib_in.at[pl.ds(section * half, half)],
-            rs_send.at[section],
-            rs_recv.at[section],
-            sibling,
-        )
+        [
+            remote(
+                part.at[pl.ds((2 * section + 1) * half, half), columns(cut)],
+                sib_in.at[pl.ds(section * half, half), columns(cut)],
+                rs_send.at[section, cut],
+                rs_recv.at[section, cut],
+                sibling,
+            )
+            for cut in range(cuts)
+        ]
         for section in range(2)
     ]
-    reduce_s[1].start()
-    reduce_s[0].start()
-    down_pass(0)
+    for src in range(line):
+        s_copy(0, src).wait_recv()
+    up_pass(0)
+    for d in range(max(line - 2, 0), line):
+        at_distance(d, from_y)
+    loads[10].wait()
+    for cut in range(cuts):
+        down_pass(0, cut)
+        reduce_s[0][cut].start()
+    for src in range(line):
+        s_copy(1, src).wait_recv()
+    up_pass(2 * half)
+    for cut in range(cuts):
+        down_pass(2 * half, cut)
+        reduce_s[1][cut].start()
 
     def target(k):
         return lax.rem(z + k, line)
 
     reduce_y = [
-        remote(
-            pair_out.at[block(0, target(k))],
-            y_in.at[block(0, target(k))],
-            ry_send.at[k],
-            ry_recv.at[k],
-            y_peer,
-        )
+        [
+            remote(
+                pair_out.at[block(0, target(k)), columns(cut)],
+                y_in.at[block(0, target(k)), columns(cut)],
+                ry_send.at[k, cut],
+                ry_recv.at[k, cut],
+                y_peer,
+            )
+            for cut in range(cuts)
+        ]
         for k in range(line)
     ]
     reduce_z = [
-        remote(
-            y_out.at[block(0, target(k))],
-            z_in.at[block(0, k)],
-            rz_send.at[k],
-            rz_recv.at[k],
-            target(k) * 4 + within,
-        )
+        [
+            remote(
+                y_out.at[block(0, target(k)), columns(cut)],
+                z_in.at[block(0, k), columns(cut)],
+                rz_send.at[k, cut],
+                rz_recv.at[k, cut],
+                target(k) * 4 + within,
+            )
+            for cut in range(cuts)
+        ]
         for k in range(1, line)
     ]
-    order = list(range(1, line)) + [0]
-    reduce_s[1].wait_recv()
-    for k in order:
-        far = block(1, target(k))
-        pair_out[block(0, target(k)), :] = (
-            part[far, :].astype(f32) + sib_in[far, :].astype(f32)
+
+    def to_y(k, cut):
+        cols = columns(cut)
+        mine, theirs = block(2, target(k)), block(1, target(k))
+        pair_out[block(0, target(k)), cols] = (
+            part[mine, cols].astype(f32) + sib_in[theirs, cols].astype(f32)
         ).astype(bf16)
-        reduce_y[k].start()
-    reduce_s[0].wait_recv()
-    for k in range(1, line):
-        here = block(0, target(k))
-        reduce_y[k].wait_recv()
-        y_out[here, :] = (
-            part[here, :].astype(f32) + sib_in[here, :].astype(f32) + y_in[here, :].astype(f32)
-        ).astype(bf16)
-        reduce_z[k - 1].start()
-    here = block(0, z)
-    reduce_y[0].wait_recv()
+        reduce_y[k][cut].start()
+
+    for cut in range(cuts):
+        reduce_s[1][cut].wait_recv()
+        for k in range(1, line):
+            to_y(k, cut)
+    for cut in range(cuts):
+        to_y(0, cut)
+    for cut in range(cuts):
+        cols = columns(cut)
+        reduce_s[0][cut].wait_recv()
+        for k in range(1, line):
+            here = block(0, target(k))
+            reduce_y[k][cut].wait_recv()
+            y_out[here, cols] = (
+                part[here, cols].astype(f32)
+                + sib_in[here, cols].astype(f32)
+                + y_in[here, cols].astype(f32)
+            ).astype(bf16)
+            reduce_z[k - 1][cut].start()
+    for cut in range(cuts):
+        reduce_y[0][cut].wait_recv()
     total = (
         x_all[own, :feat].astype(f32)
-        + part[here, :].astype(f32)
-        + sib_in[here, :].astype(f32)
-        + y_in[here, :].astype(f32)
+        + part[own, :].astype(f32)
+        + sib_in[own, :].astype(f32)
+        + y_in[own, :].astype(f32)
     )
     for k in range(1, line):
-        reduce_z[k - 1].wait_recv()
+        for cut in range(cuts):
+            reduce_z[k - 1][cut].wait_recv()
         total = total + z_in[k * rows : (k + 1) * rows, :].astype(f32)
     hidden = total.astype(bf16).astype(f32)
     scale = lax.rsqrt(jnp.mean(hidden * hidden, axis=-1, keepdims=True) + 1e-06)
@@ -423,10 +469,15 @@
             voice = base_voice[f, :, cols] + gain * owned
             voice_ref[f, :, cols] = jnp.where(count > f, voice, 0.0).astype(bf16)
 
-    for copy in (
-        gather_z + gather_y + gather_s[0] + gather_s[1] + reduce_s + reduce_y + reduce_z + exchange
-    ):
-        copy.wait_send()
+    for d in range(line):
+        pass_z(d, lambda copy: copy.wait_send())
+    for src in range(line):
+        y_copy(src).wait_send()
+        s_copy(0, src).wait_send()
+        s_copy(1, src).wait_send()
+    for group in reduce_s + reduce_y + reduce_z + [exchange]:
+        for copy in group:
+            copy.wait_send()
 
 
 def dense_path(
@@ -454,6 +505,7 @@
     chosen = expert_ids.shape[1]
     before = left_context.shape[1]
     horizon = frame_offset.shape[0]
+    cuts = 2
     vmem = pl.BlockSpec(memory_space=pltpu.VMEM)
     hbm = pl.BlockSpec(memory_space=pl.ANY)
     dma = pltpu.SemaphoreType.DMA
@@ -486,18 +538,18 @@
             pltpu.VMEM((n, width // LANES, LANES), f32),
             pltpu.VMEM((n, width // LANES, LANES), f32),
             dma((12,)),
-            dma((line,)),
+            dma((2, line)),
             dma((line,)),
             dma((line,)),
             dma((line,)),
             dma((2, line)),
             dma((2, line)),
-            dma((2,)),
-            dma((2,)),
-            dma((line,)),
-            dma((line,)),
-            dma((line,)),
-            dma((line,)),
+            dma((2, cuts)),
+            dma((2, cuts)),
+            dma((line, cuts)),
+            dma((line, cuts)),
+            dma((line, cuts)),
+            dma((line, cuts)),
             dma((n,)),
             dma((n,)),
         ],

time: 42.4 us -> 43 us (1.014)
  Pallas kernels: 40.5 us -> 41.2 us
    pallas_call x1, Pallas kernels: 40.5 us -> 41.2 us  [dense_path(): pl.pallas_call(functools.partial(dense_kernel, n), out_shape=jax.ShapeDty...]
where the time goes in v3:
time: 43 us; the launch traced here: 42.9 us
  Pallas kernels  41.2 us (96%)
  local copies, waits for them, and re-layouts  1.66 us (4%)
    pallas_call x1, Pallas kernels, dense_path(): pl.pallas_call(functools.partial(dense_kernel, n), out_shape=jax.ShapeDty...  41.2 us
    transpose x1, local copies, waits for them, and re-layouts, dense_path(): return voice.transpose(1, 0, 2)  1.66 us

profile of v3, /device:TPU:0, one launch (start us, length us, event | category | flops | bytes accessed | tf_op | source)
XLA Modules:
  0.0 42.9 jit_solution(1802871417157786888)
XLA Ops:
  0.0 41.2 %shard_map.118 = bf16[4,16,1024]{2,1,0:T(8,128)(2,1)} custom-call(bf16[16,2048]{1,0:T(8,128)(2,1)} %rows_hbm.1, s32[8,16]{1,0:T(8,128)} %bitcast.7, f32[8,16]{1,0:T(8,128)} %bitcast.8, s32[1,16]{1,0:T(1,128)} %slot_hbm.1, s32[1,16]{1,0:T(1,128)} %bitcast.9, bf16[6,16,1024]{2,1,0:T(8,128)(2,1)} %bitcast.6, f32[4,1024]{1,0:T(4,128)} %offset_hbm.1, ...), custom_call_target="tpu_custom_call" | custom-call | tf_op jit(solution)/shard_map/pallas_call | solution.py:512
  41.2 1.7 %copy.13 = bf16[16,4,1024]{2,1,0:T(4,128)(2,1)} copy(bf16[16,4,1024]{2,0,1:T(8,128)(2,1)} %bitcast.5) | data formatting | bytes 262144 | tf_op jit(solution)/shard_map/transpose | solution.py:573

commit v4 on v3

--- a/solution.py
+++ b/solution.py
@@ -111,6 +111,7 @@
     wd_hbm,
     proj_hbm,
     voice_ref,
+    rows_ref,
     ids_ref,
     gates_ref,
     slot_ref,
@@ -125,14 +126,13 @@
     proj,
     x_all,
     inner,
+    grouped,
     part,
     sib_in,
     pair_out,
     y_in,
     y_out,
     z_in,
-    row_out,
-    row_in,
     load_sem,
     gz_send,
     gz_recv,
@@ -146,8 +146,6 @@
     ry_recv,
     rz_send,
     rz_recv,
-    t_send,
-    t_recv,
 ):
     f32, bf16 = jnp.float32, jnp.bfloat16
     rows, feat = rows_hbm.shape
@@ -172,7 +170,7 @@
         pltpu.make_async_copy(src, dst, load_sem.at[i])
         for i, (src, dst) in enumerate(
             (
-                (rows_hbm, x_all.at[own, pl.ds(0, feat)]),
+                (rows_hbm, rows_ref),
                 (ids_hbm, ids_ref),
                 (gates_hbm, gates_ref),
                 (slot_hbm, slot_ref),
@@ -187,18 +185,20 @@
             )
         )
     ]
-    for load in loads:
+    for load in loads[:4]:
         load.start()
 
+    z_peers = [lax.rem(z + k, line) * 4 + within for k in range(1, line)]
+    partners = z_peers + [y_peer, sibling]
     barrier = pltpu.get_barrier_semaphore()
-    for k in range(1, n):
-        pl.semaphore_signal(barrier, inc=1, device_id={"ep": lax.rem(me + k, n)})
+    for peer in partners:
+        pl.semaphore_signal(barrier, inc=1, device_id={"ep": peer})
 
     extra = x_all.shape[1] - feat
     spot = lax.broadcasted_iota(jnp.int32, (extra, rows), 0)
     expert_of = lax.rem(spot, n)
     weight = jnp.zeros((extra, rows), f32)
-    for load in loads[:5]:
+    for load in loads[:4]:
         load.wait()
     for j in range(ids_ref.shape[0]):
         weight = weight + jnp.where(
@@ -208,27 +208,23 @@
     mid = (weight - high).astype(bf16).astype(f32)
     low = weight - high - mid
     coded = jnp.where(spot < n, high, jnp.where(spot < 2 * n, mid, jnp.where(spot < 3 * n, low, 0.0)))
-    diagonal = lax.broadcasted_iota(jnp.int32, (rows, rows), 0) == lax.broadcasted_iota(
-        jnp.int32, (rows, rows), 1
-    )
+    owner = lax.broadcasted_iota(jnp.int32, (n, rows), 0)
+    pick = jnp.where(owner == slot_ref[...], 1.0, 0.0).astype(bf16)
+    x_all[own, :feat] = jnp.dot(pick, rows_ref[...], preferred_element_type=f32).astype(bf16)
     x_all[own, feat:] = lax.dot_general(
-        jnp.where(diagonal, 1.0, 0.0).astype(bf16),
-        coded.astype(bf16),
-        (((1,), (1,)), ((), ())),
-        preferred_element_type=f32,
+        pick, coded.astype(bf16), (((1,), (1,)), ((), ())), preferred_element_type=f32
     ).astype(bf16)
 
-    pl.semaphore_wait(barrier, n - 1)
+    pl.semaphore_wait(barrier, len(partners))
 
     def remote(src, dst, send, recv, peer):
         return pltpu.make_async_remote_copy(
             src_ref=src, dst_ref=dst, send_sem=send, recv_sem=recv, device_id={"ep": peer}
         )
 
-    def z_copy(up, src):
+    def z_copy(peer, src):
         here = x_all.at[block(0, src)]
-        step = 4 if up else -4
-        return remote(here, here, gz_send.at[int(up), src], gz_recv.at[src], me + step)
+        return remote(here, here, gz_send.at[peer], gz_recv.at[src], peer * 4 + within)
 
     def y_copy(src):
         return remote(
@@ -252,19 +248,11 @@
         for src in (z,) if d == 0 else (z - d, z + d):
             pl.when((src >= 0) & (src < line))(functools.partial(use, src))
 
-    def pass_z(d, act):
-        def go(up, src):
-            pl.when((z + 1 < line) if up else (z > 0))(lambda: act(z_copy(up, src)))
-
-        if d == 0:
-            go(True, z)
-            go(False, z)
-        else:
-            pl.when(z - d >= 0)(lambda: go(True, z - d))
-            pl.when(z + d < line)(lambda: go(False, z + d))
+    def to_z(d, act):
+        at_distance(d, lambda peer: act(z_copy(peer, z)))
 
     def from_z(d):
-        at_distance(d, lambda src: z_copy(True, src).wait_recv())
+        at_distance(d, lambda src: z_copy(src, src).wait_recv())
 
     def hand_on(src):
         y_copy(src).start()
@@ -274,10 +262,14 @@
         y_copy(src).wait_recv()
         s_copy(1, src).start()
 
-    pass_z(0, lambda copy: copy.start())
+    to_z(1, lambda copy: copy.start())
     hand_on(z)
-
-    for load in loads[5:8]:
+    for d in range(2, line):
+        to_z(d, lambda copy: copy.start())
+    for load in loads[4:]:
+        load.start()
+
+    for load in loads[4:8]:
         load.wait()
     before = context.shape[0]
     horizon = frame_offset.shape[0]
@@ -293,7 +285,6 @@
 
     for d in range(1, line):
         from_z(d)
-        pass_z(d, lambda copy: copy.start())
         at_distance(d, hand_on)
         if d < line - 1:
             at_distance(d - 1, from_y)
@@ -303,29 +294,45 @@
 
     def up_pass(base):
         span = pl.ds(base, 2 * half)
+        lanes = lax.broadcasted_iota(jnp.int32, (2 * half, extra), 1)
+        mine = (lax.rem(lanes, n) == me) & (lanes < 3 * n)
+        coef = jnp.sum(
+            jnp.where(mine, x_all[span, feat:].astype(f32), 0.0), axis=1, keepdims=True
+        )
 
         def step(j, carry):
             cols = pl.ds(pl.multiple_of(j * tile, tile), tile)
             x = x_all[span, :feat]
             gate_act = jnp.dot(x, wg[:, cols], preferred_element_type=f32)
             up_act = jnp.dot(x, wu[:, cols], preferred_element_type=f32)
-            inner[span, cols] = (jax.nn.silu(gate_act) * up_act).astype(bf16)
+            inner[span, cols] = (jax.nn.silu(gate_act) * up_act * coef).astype(bf16)
             return carry
 
         lax.fori_loop(0, hid // tile, step, 0)
+
+    def place(index):
+        section = index // half
+        device = (
+            (index % half) // rows * 4
+            + jnp.where(section // 2 == 0, y, 1 - y) * 2
+            + jnp.where(section % 2 == 0, core, 1 - core)
+        )
+        return device, index % rows
+
+    def regroup():
+        every = n * rows
+        row_owner, row_source = place(lax.broadcasted_iota(jnp.int32, (every, 1), 0))
+        col_source, col_owner = place(lax.broadcasted_iota(jnp.int32, (1, every), 1))
+        match = (row_owner == col_owner) & (row_source == col_source)
+        return jnp.where(match, 1.0, 0.0).astype(bf16)
 
     def down_pass(base, cut):
         span = pl.ds(base, 2 * half)
-        lanes = lax.broadcasted_iota(jnp.int32, (2 * half, extra), 1)
-        mine = (lax.rem(lanes, n) == me) & (lanes < 3 * n)
-        coef = jnp.sum(
-            jnp.where(mine, x_all[span, feat:].astype(f32), 0.0), axis=1, keepdims=True
-        )
 
         def step(j, carry):
             cols = pl.ds(pl.multiple_of(cut * piece + j * tile, tile), tile)
-            out = jnp.dot(inner[span, :], wd[:, cols], preferred_element_type=f32)
-            part[span, cols] = (out * coef).astype(bf16)
+            out = jnp.dot(grouped[span, :], wd[:, cols], preferred_element_type=f32)
+            part[span, cols] = out.astype(bf16)
             return carry
 
         lax.fori_loop(0, piece // tile, step, 0)
@@ -354,16 +361,20 @@
     up_pass(0)
     for d in range(max(line - 2, 0), line):
         at_distance(d, from_y)
-    loads[10].wait()
-    for cut in range(cuts):
-        down_pass(0, cut)
-        reduce_s[0][cut].start()
+    order = regroup()
     for src in range(line):
         s_copy(1, src).wait_recv()
     up_pass(2 * half)
-    for cut in range(cuts):
-        down_pass(2 * half, cut)
-        reduce_s[1][cut].start()
+    grouped[...] = jnp.dot(order, inner[...], preferred_element_type=f32).astype(bf16)
+    loads[10].wait()
+    for section in (1, 0):
+        for cut in range(cuts):
+            down_pass(section * 2 * half, cut)
+            reduce_s[section][cut].start()
+
+    col_source, col_owner = place(lax.broadcasted_iota(jnp.int32, (1, n * rows), 1))
+    source = lax.broadcasted_iota(jnp.int32, (rows, 1), 0)
+    keep = jnp.where((col_source == source) & (col_owner == me), 1.0, 0.0).astype(bf16)
 
     def target(k):
         return lax.rem(z + k, line)
@@ -421,10 +432,11 @@
                 + y_in[here, cols].astype(f32)
             ).astype(bf16)
             reduce_z[k - 1][cut].start()
+    residual = jnp.dot(keep, x_all[:, :feat], preferred_element_type=f32)
     for cut in range(cuts):
         reduce_y[0][cut].wait_recv()
     total = (
-        x_all[own, :feat].astype(f32)
+        residual
         + part[own, :].astype(f32)
         + sib_in[own, :].astype(f32)
         + y_in[own, :].astype(f32)
@@ -437,45 +449,29 @@
     scale = lax.rsqrt(jnp.mean(hidden * hidden, axis=-1, keepdims=True) + 1e-06)
     normed = (hidden * scale).astype(bf16)
 
-    owner = lax.broadcasted_iota(jnp.int32, (n, rows), 0)
-    pick = jnp.where(owner == slot_ref[...], 1.0, 0.0).astype(bf16)
     loads[11].wait()
-    for j in range(width // tile):
-        talk = jnp.dot(
-            normed, proj[:, j * tile : (j + 1) * tile], preferred_element_type=f32
-        ).astype(bf16)
-        ordered = jnp.dot(pick, talk, preferred_element_type=f32)
-        for i in range(tile // LANES):
-            row_out[:, j * (tile // LANES) + i, :] = ordered[:, i * LANES : (i + 1) * LANES]
-    exchange = []
-    for k in range(1, n):
-        peer = lax.rem(me + k, n)
-        exchange.append(
-            remote(row_out.at[peer], row_in.at[me], t_send.at[k], t_recv.at[k], peer)
-        )
-    for copy in exchange:
-        copy.start()
-    row_in[pl.ds(me, 1)] = row_out[pl.ds(me, 1)]
-    for copy in exchange:
-        copy.wait_recv()
+    diagonal = lax.broadcasted_iota(jnp.int32, (rows, rows), 0) == lax.broadcasted_iota(
+        jnp.int32, (rows, rows), 1
+    )
     count = jnp.sum(
         jnp.where(diagonal, count_ref[...].astype(f32), 0.0), axis=1, keepdims=True
     )
-    for i in range(width // LANES):
-        cols = slice(i * LANES, (i + 1) * LANES)
-        owned = row_in[:, i, :]
+    for j in range(width // tile):
+        cols = slice(j * tile, (j + 1) * tile)
+        talk = jnp.dot(normed, proj[:, cols], preferred_element_type=f32)
+        owned = talk.astype(bf16).astype(f32)
         for f in range(horizon):
             gain = jnp.sum(taps[before - f :, cols], axis=0, keepdims=True)
             voice = base_voice[f, :, cols] + gain * owned
             voice_ref[f, :, cols] = jnp.where(count > f, voice, 0.0).astype(bf16)
 
-    for d in range(line):
-        pass_z(d, lambda copy: copy.wait_send())
+    for d in range(1, line):
+        to_z(d, lambda copy: copy.wait_send())
     for src in range(line):
         y_copy(src).wait_send()
         s_copy(0, src).wait_send()
         s_copy(1, src).wait_send()
-    for group in reduce_s + reduce_y + reduce_z + [exchange]:
+    for group in reduce_s + reduce_y + reduce_z:
         for copy in group:
             copy.wait_send()
 
@@ -515,6 +511,7 @@
         in_specs=[hbm] * 12,
         out_specs=vmem,
         scratch_shapes=[
+            pltpu.VMEM((rows, feat), bf16),
             pltpu.VMEM((chosen, rows), jnp.int32),
             pltpu.VMEM((chosen, rows), f32),
             pltpu.VMEM((1, rows), jnp.int32),
@@ -529,16 +526,15 @@
             pltpu.VMEM((feat, width), bf16),
             pltpu.VMEM((every, feat + extra), bf16),
             pltpu.VMEM((every, hid), bf16),
+            pltpu.VMEM((every, hid), bf16),
             pltpu.VMEM((every, feat), bf16),
             pltpu.VMEM((every // 2, feat), bf16),
             pltpu.VMEM((line * rows, feat), bf16),
             pltpu.VMEM((line * rows, feat), bf16),
             pltpu.VMEM((line * rows, feat), bf16),
             pltpu.VMEM((line * rows, feat), bf16),
-            pltpu.VMEM((n, width // LANES, LANES), f32),
-            pltpu.VMEM((n, width // LANES, LANES), f32),
             dma((12,)),
-            dma((2, line)),
+            dma((line,)),
             dma((line,)),
             dma((line,)),
             dma((line,)),
@@ -550,8 +546,6 @@
             dma((line, cuts)),
             dma((line, cuts)),
             dma((line, cuts)),
-            dma((n,)),
-            dma((n,)),
         ],
         compiler_params=pltpu.CompilerParams(
             collective_id=0, has_side_effects=True, vmem_limit_bytes=60 * 1024 * 1024

time: 43 us -> 34.2 us (0.80)
  Pallas kernels: 41.2 us -> 32.3 us
    pallas_call x1, Pallas kernels: 41.2 us -> 32.3 us  [dense_path(): pl.pallas_call(functools.partial(dense_kernel, n), out_shape=jax.ShapeDty...]
where the time goes in v4:
time: 34.2 us; the launch traced here: 34 us
  Pallas kernels  32.3 us (94%)
  local copies, waits for them, and re-layouts  1.66 us (5%)
    pallas_call x1, Pallas kernels, dense_path(): pl.pallas_call(functools.partial(dense_kernel, n), out_shape=jax.ShapeDty...  32.3 us
    transpose x1, local copies, waits for them, and re-layouts, dense_path(): return voice.transpose(1, 0, 2)  1.66 us

profile of v4, /device:TPU:0, one launch (start us, length us, event | category | flops | bytes accessed | tf_op | source)
XLA Modules:
  0.0 34.0 jit_solution(5483355990692289974)
XLA Ops:
  0.0 32.3 %shard_map.118 = bf16[4,16,1024]{2,1,0:T(8,128)(2,1)} custom-call(bf16[16,2048]{1,0:T(8,128)(2,1)} %rows_hbm.1, s32[8,16]{1,0:T(8,128)} %bitcast.7, f32[8,16]{1,0:T(8,128)} %bitcast.8, s32[1,16]{1,0:T(1,128)} %slot_hbm.1, s32[1,16]{1,0:T(1,128)} %bitcast.9, bf16[6,16,1024]{2,1,0:T(8,128)(2,1)} %bitcast.6, f32[4,1024]{1,0:T(4,128)} %offset_hbm.1, ...), custom_call_target="tpu_custom_call" | custom-call | tf_op jit(solution)/shard_map/pallas_call | solution.py:508
  32.3 1.7 %copy.13 = bf16[16,4,1024]{2,1,0:T(4,128)(2,1)} copy(bf16[16,4,1024]{2,0,1:T(8,128)(2,1)} %bitcast.5) | data formatting | bytes 262144 | tf_op jit(solution)/shard_map/transpose | solution.py:567

commit v5 on v4

--- a/solution.py
+++ b/solution.py
@@ -120,6 +120,7 @@
     frame_offset,
     taps,
     base_voice,
+    voices,
     wg,
     wu,
     wd,
@@ -367,10 +368,9 @@
     up_pass(2 * half)
     grouped[...] = jnp.dot(order, inner[...], preferred_element_type=f32).astype(bf16)
     loads[10].wait()
-    for section in (1, 0):
-        for cut in range(cuts):
-            down_pass(section * 2 * half, cut)
-            reduce_s[section][cut].start()
+    for cut in range(cuts):
+        down_pass(2 * half, cut)
+        reduce_s[1][cut].start()
 
     col_source, col_owner = place(lax.broadcasted_iota(jnp.int32, (1, n * rows), 1))
     source = lax.broadcasted_iota(jnp.int32, (rows, 1), 0)
@@ -415,6 +415,8 @@
         reduce_y[k][cut].start()
 
     for cut in range(cuts):
+        down_pass(0, cut)
+        reduce_s[0][cut].start()
         reduce_s[1][cut].wait_recv()
         for k in range(1, line):
             to_y(k, cut)
@@ -463,7 +465,8 @@
         for f in range(horizon):
             gain = jnp.sum(taps[before - f :, cols], axis=0, keepdims=True)
             voice = base_voice[f, :, cols] + gain * owned
-            voice_ref[f, :, cols] = jnp.where(count > f, voice, 0.0).astype(bf16)
+            voices[:, f, cols] = jnp.where(count > f, voice, 0.0)
+        voice_ref[:, :, cols] = voices[:, :, cols].astype(bf16)
 
     for d in range(1, line):
         to_z(d, lambda copy: copy.wait_send())
@@ -505,9 +508,9 @@
     vmem = pl.BlockSpec(memory_space=pltpu.VMEM)
     hbm = pl.BlockSpec(memory_space=pl.ANY)
     dma = pltpu.SemaphoreType.DMA
-    voice = pl.pallas_call(
+    return pl.pallas_call(
         functools.partial(dense_kernel, n),
-        out_shape=jax.ShapeDtypeStruct((horizon, rows, width), bf16),
+        out_shape=jax.ShapeDtypeStruct((rows, horizon, width), bf16),
         in_specs=[hbm] * 12,
         out_specs=vmem,
         scratch_shapes=[
@@ -520,6 +523,7 @@
             pltpu.VMEM((horizon, width), f32),
             pltpu.VMEM(conv_weight.shape, f32),
             pltpu.VMEM((horizon, rows, width), f32),
+            pltpu.VMEM((rows, horizon, width), f32),
             pltpu.VMEM((feat, hid), bf16),
             pltpu.VMEM((feat, hid), bf16),
             pltpu.VMEM((hid, feat), bf16),
@@ -564,7 +568,6 @@
         w_down,
         talker_proj,
     )
-    return voice.transpose(1, 0, 2)
 
 
 def local(

time: 34.2 us -> 34.1 us (level)
    transpose x1 -> x0, local copies, waits for them, and re-layouts: 1.66 us -> none  [dense_path(): return voice.transpose(1, 0, 2)]
    unnamed x0 -> x1, local copies, waits for them, and re-layouts: none -> 1.61 us
where the time goes in v5:
time: 34.1 us; the launch traced here: 33.9 us
  Pallas kernels  32.3 us (95%)
  local copies, waits for them, and re-layouts  1.61 us (5%)
    pallas_call x1, Pallas kernels, dense_path(): pl.pallas_call(functools.partial(dense_kernel, n), out_shape=jax.ShapeDty...  32.3 us
    unnamed x1, local copies, waits for them, and re-layouts  1.61 us

profile of v5, /device:TPU:0, one launch (start us, length us, event | category | flops | bytes accessed | tf_op | source)
XLA Modules:
  0.0 33.9 jit_solution(3558038166337012879)
XLA Ops:
  0.0 32.3 %shard_map.118 = bf16[16,4,1024]{2,1,0:T(4,128)(2,1)} custom-call(bf16[16,2048]{1,0:T(8,128)(2,1)} %rows_hbm.1, s32[8,16]{1,0:T(8,128)} %bitcast.5, f32[8,16]{1,0:T(8,128)} %bitcast.6, s32[1,16]{1,0:T(1,128)} %slot_hbm.1, s32[1,16]{1,0:T(1,128)} %bitcast.7, bf16[6,16,1024]{2,1,0:T(8,128)(2,1)} %bitcast.4, f32[4,1024]{1,0:T(4,128)} %offset_hbm.1, ...), custom_call_target="tpu_custom_call" | custom-call | tf_op jit(solution)/shard_map/pallas_call | solution.py:511
  32.3 1.6 %copy.14 = bf16[16,4,1024]{2,1,0:T(4,128)(2,1)} copy(bf16[16,4,1024]{2,1,0:T(4,128)(2,1)} %shard_map.118) | data formatting | bytes 262144

commit v6 on v5

--- a/solution.py
+++ b/solution.py
@@ -134,6 +134,7 @@
     y_in,
     y_out,
     z_in,
+    relay_in,
     load_sem,
     gz_send,
     gz_recv,
@@ -147,6 +148,7 @@
     ry_recv,
     rz_send,
     rz_recv,
+    relay_recv,
 ):
     f32, bf16 = jnp.float32, jnp.bfloat16
     rows, feat = rows_hbm.shape
@@ -189,6 +191,11 @@
     for load in loads[:4]:
         load.start()
 
+    @pl.when((z == 0) | (z == line - 1))
+    def _():
+        relay_in[...] = jnp.zeros_like(relay_in)
+        z_in[block(0, line - 1 - z), :] = jnp.zeros((rows, feat), bf16)
+
     z_peers = [lax.rem(z + k, line) * 4 + within for k in range(1, line)]
     partners = z_peers + [y_peer, sibling]
     barrier = pltpu.get_barrier_semaphore()
@@ -225,7 +232,8 @@
 
     def z_copy(peer, src):
         here = x_all.at[block(0, src)]
-        return remote(here, here, gz_send.at[peer], gz_recv.at[src], peer * 4 + within)
+        slot = peer if src is z else line
+        return remote(here, here, gz_send.at[slot], gz_recv.at[src], peer * 4 + within)
 
     def y_copy(src):
         return remote(
@@ -255,6 +263,10 @@
     def from_z(d):
         at_distance(d, lambda src: z_copy(src, src).wait_recv())
 
+    def relay_z(act):
+        pl.when(z == line - 2)(lambda: act(z_copy(z + 1, 0)))
+        pl.when(z == 1)(lambda: act(z_copy(z - 1, line - 1)))
+
     def hand_on(src):
         y_copy(src).start()
         s_copy(0, src).start()
@@ -265,7 +277,7 @@
 
     to_z(1, lambda copy: copy.start())
     hand_on(z)
-    for d in range(2, line):
+    for d in range(2, line - 1):
         to_z(d, lambda copy: copy.start())
     for load in loads[4:]:
         load.start()
@@ -286,6 +298,8 @@
 
     for d in range(1, line):
         from_z(d)
+        if d == line - 2:
+            relay_z(lambda copy: copy.start())
         at_distance(d, hand_on)
         if d < line - 1:
             at_distance(d - 1, from_y)
@@ -376,8 +390,15 @@
     source = lax.broadcasted_iota(jnp.int32, (rows, 1), 0)
     keep = jnp.where((col_source == source) & (col_owner == me), 1.0, 0.0).astype(bf16)
 
+    last = line - 1
+    upper = z // 2
+    inside = z * (last - z) // 2
+
     def target(k):
-        return lax.rem(z + k, line)
+        if k == 0:
+            return z
+        low = {1: last - last * inside, 2: 2, 3: 1 + 2 * inside}[k]
+        return upper * (last - low) + (1 - upper) * low
 
     reduce_y = [
         [
@@ -396,15 +417,28 @@
         [
             remote(
                 y_out.at[block(0, target(k)), columns(cut)],
-                z_in.at[block(0, k), columns(cut)],
+                z_in.at[own, columns(cut)],
                 rz_send.at[k, cut],
-                rz_recv.at[k, cut],
+                rz_recv.at[z, cut],
                 target(k) * 4 + within,
             )
             for cut in range(cuts)
         ]
         for k in range(1, line)
     ]
+
+    def relay(cut):
+        return remote(
+            y_out.at[block(0, target(1)), columns(cut)],
+            relay_in.at[:, columns(cut)],
+            rz_send.at[1, cut],
+            relay_recv.at[cut],
+            (1 + upper) * 4 + within,
+        )
+
+    def arrived_z(src, cut):
+        here = z_in.at[block(0, src), columns(cut)]
+        remote(here, here, rz_send.at[0, cut], rz_recv.at[src, cut], sibling).wait_recv()
 
     def to_y(k, cut):
         cols = columns(cut)
@@ -428,12 +462,20 @@
         for k in range(1, line):
             here = block(0, target(k))
             reduce_y[k][cut].wait_recv()
-            y_out[here, cols] = (
+            partial = (
                 part[here, cols].astype(f32)
                 + sib_in[here, cols].astype(f32)
                 + y_in[here, cols].astype(f32)
-            ).astype(bf16)
-            reduce_z[k - 1][cut].start()
+            )
+            if k == last:
+                pl.when(inside == 1)(lambda cut=cut: relay(cut).wait_recv())
+                partial = partial + relay_in[:, cols].astype(f32)
+            y_out[here, cols] = partial.astype(bf16)
+            if k == 1:
+                pl.when(inside == 0)(lambda cut=cut: relay(cut).start())
+                pl.when(inside == 1)(lambda cut=cut: reduce_z[0][cut].start())
+            else:
+                reduce_z[k - 1][cut].start()
     residual = jnp.dot(keep, x_all[:, :feat], preferred_element_type=f32)
     for cut in range(cuts):
         reduce_y[0][cut].wait_recv()
@@ -444,9 +486,11 @@
         + y_in[own, :].astype(f32)
     )
     for k in range(1, line):
+        src = lax.rem(z + k, line)
         for cut in range(cuts):
-            reduce_z[k - 1][cut].wait_recv()
-        total = total + z_in[k * rows : (k + 1) * rows, :].astype(f32)
+            direct = (inside == 1) | (src + z != last)
+            pl.when(direct)(functools.partial(arrived_z, src, cut))
+        total = total + z_in[block(0, src), :].astype(f32)
     hidden = total.astype(bf16).astype(f32)
     scale = lax.rsqrt(jnp.mean(hidden * hidden, axis=-1, keepdims=True) + 1e-06)
     normed = (hidden * scale).astype(bf16)
@@ -468,8 +512,9 @@
             voices[:, f, cols] = jnp.where(count > f, voice, 0.0)
         voice_ref[:, :, cols] = voices[:, :, cols].astype(bf16)
 
-    for d in range(1, line):
+    for d in range(1, line - 1):
         to_z(d, lambda copy: copy.wait_send())
+    relay_z(lambda copy: copy.wait_send())
     for src in range(line):
         y_copy(src).wait_send()
         s_copy(0, src).wait_send()
@@ -537,8 +582,9 @@
             pltpu.VMEM((line * rows, feat), bf16),
             pltpu.VMEM((line * rows, feat), bf16),
             pltpu.VMEM((line * rows, feat), bf16),
+            pltpu.VMEM((rows, feat), bf16),
             dma((12,)),
-            dma((line,)),
+            dma((line + 1,)),
             dma((line,)),
             dma((line,)),
             dma((line,)),
@@ -550,6 +596,7 @@
             dma((line, cuts)),
             dma((line, cuts)),
             dma((line, cuts)),
+            dma((cuts,)),
         ],
         compiler_params=pltpu.CompilerParams(
             collective_id=0, has_side_effects=True, vmem_limit_bytes=60 * 1024 * 1024
@@ -586,7 +633,7 @@
 ):
     devices = lax.axis_size("ep")
     streams_here = thinker_rows.shape[0]
-    dense = streams_here <= CAP and streams_here == devices and devices % 4 == 0
+    dense = streams_here <= CAP and streams_here == devices and devices == 4 * 4
     experts = (
         thinker_rows, expert_ids, gate_weights, w_gate, w_up, w_down, talker_proj, talker_slot
     )

time: 34.1 us -> 36.5 us (1.070)
  Pallas kernels: 32.3 us -> 34.7 us
    pallas_call x1, Pallas kernels: 32.3 us -> 34.7 us  [dense_path(): pl.pallas_call(functools.partial(dense_kernel, n), out_shape=jax.ShapeDty...]
where the time goes in v6:
time: 36.5 us; the launch traced here: 36.3 us
  Pallas kernels  34.7 us (95%)
  local copies, waits for them, and re-layouts  1.61 us (4%)
    pallas_call x1, Pallas kernels, dense_path(): pl.pallas_call(functools.partial(dense_kernel, n), out_shape=jax.ShapeDty...  34.7 us
    unnamed x1, local copies, waits for them, and re-layouts  1.61 us

profile of v6, /device:TPU:0, one launch (start us, length us, event | category | flops | bytes accessed | tf_op | source)
XLA Modules:
  0.0 36.3 jit_solution(12917827171048681705)
XLA Ops:
  0.0 34.7 %shard_map.118 = bf16[16,4,1024]{2,1,0:T(4,128)(2,1)} custom-call(bf16[16,2048]{1,0:T(8,128)(2,1)} %rows_hbm.1, s32[8,16]{1,0:T(8,128)} %bitcast.5, f32[8,16]{1,0:T(8,128)} %bitcast.6, s32[1,16]{1,0:T(1,128)} %slot_hbm.1, s32[1,16]{1,0:T(1,128)} %bitcast.7, bf16[6,16,1024]{2,1,0:T(8,128)(2,1)} %bitcast.4, f32[4,1024]{1,0:T(4,128)} %offset_hbm.1, ...), custom_call_target="tpu_custom_call" | custom-call | tf_op jit(solution)/shard_map/pallas_call | solution.py:556
  34.7 1.6 %copy.14 = bf16[16,4,1024]{2,1,0:T(4,128)(2,1)} copy(bf16[16,4,1024]{2,1,0:T(4,128)(2,1)} %shard_map.118) | data formatting | bytes 262144

commit v7 on v5

--- a/solution.py
+++ b/solution.py
@@ -120,6 +120,9 @@
     frame_offset,
     taps,
     base_voice,
+    gains,
+    order,
+    keep,
     voices,
     wg,
     wu,
@@ -223,6 +226,27 @@
             src_ref=src, dst_ref=dst, send_sem=send, recv_sem=recv, device_id={"ep": peer}
         )
 
+    def place(index):
+        section = index // half
+        device = (
+            (index % half) // rows * 4
+            + jnp.where(section // 2 == 0, y, 1 - y) * 2
+            + jnp.where(section % 2 == 0, core, 1 - core)
+        )
+        return device, index % rows
+
+    def regroup():
+        every = n * rows
+        row_owner, row_source = place(lax.broadcasted_iota(jnp.int32, (every, 1), 0))
+        col_source, col_owner = place(lax.broadcasted_iota(jnp.int32, (1, every), 1))
+        match = (row_owner == col_owner) & (row_source == col_source)
+        return jnp.where(match, 1.0, 0.0).astype(bf16)
+
+    def owned_rows():
+        col_source, col_owner = place(lax.broadcasted_iota(jnp.int32, (1, n * rows), 1))
+        source = lax.broadcasted_iota(jnp.int32, (rows, 1), 0)
+        return jnp.where((col_source == source) & (col_owner == me), 1.0, 0.0).astype(bf16)
+
     def z_copy(peer, src):
         here = x_all.at[block(0, src)]
         return remote(here, here, gz_send.at[peer], gz_recv.at[src], peer * 4 + within)
@@ -270,19 +294,8 @@
     for load in loads[4:]:
         load.start()
 
-    for load in loads[4:8]:
-        load.wait()
-    before = context.shape[0]
-    horizon = frame_offset.shape[0]
-    for f in range(horizon):
-        voice = jnp.zeros((rows, width), f32)
-        for t in range(taps.shape[0]):
-            tap = taps[t : t + 1, :]
-            if f + t < before:
-                voice = voice + tap * context[f + t].astype(f32)
-            else:
-                voice = voice + tap * frame_offset[f + t - before : f + t - before + 1, :]
-        base_voice[f] = voice
+    order[...] = regroup()
+    keep[...] = owned_rows()
 
     for d in range(1, line):
         from_z(d)
@@ -293,7 +306,7 @@
     loads[8].wait()
     loads[9].wait()
 
-    def up_pass(base):
+    def up_pass(base, first, stop):
         span = pl.ds(base, 2 * half)
         lanes = lax.broadcasted_iota(jnp.int32, (2 * half, extra), 1)
         mine = (lax.rem(lanes, n) == me) & (lanes < 3 * n)
@@ -309,23 +322,7 @@
             inner[span, cols] = (jax.nn.silu(gate_act) * up_act * coef).astype(bf16)
             return carry
 
-        lax.fori_loop(0, hid // tile, step, 0)
-
-    def place(index):
-        section = index // half
-        device = (
-            (index % half) // rows * 4
-            + jnp.where(section // 2 == 0, y, 1 - y) * 2
-            + jnp.where(section % 2 == 0, core, 1 - core)
-        )
-        return device, index % rows
-
-    def regroup():
-        every = n * rows
-        row_owner, row_source = place(lax.broadcasted_iota(jnp.int32, (every, 1), 0))
-        col_source, col_owner = place(lax.broadcasted_iota(jnp.int32, (1, every), 1))
-        match = (row_owner == col_owner) & (row_source == col_source)
-        return jnp.where(match, 1.0, 0.0).astype(bf16)
+        lax.fori_loop(first, stop, step, 0)
 
     def down_pass(base, cut):
         span = pl.ds(base, 2 * half)
@@ -359,22 +356,19 @@
     ]
     for src in range(line):
         s_copy(0, src).wait_recv()
-    up_pass(0)
+    steps = hid // tile
+    up_pass(0, 0, steps // 2)
     for d in range(max(line - 2, 0), line):
         at_distance(d, from_y)
-    order = regroup()
+    up_pass(0, steps // 2, steps)
     for src in range(line):
         s_copy(1, src).wait_recv()
-    up_pass(2 * half)
-    grouped[...] = jnp.dot(order, inner[...], preferred_element_type=f32).astype(bf16)
+    up_pass(2 * half, 0, steps)
+    grouped[...] = jnp.dot(order[...], inner[...], preferred_element_type=f32).astype(bf16)
     loads[10].wait()
     for cut in range(cuts):
         down_pass(2 * half, cut)
         reduce_s[1][cut].start()
-
-    col_source, col_owner = place(lax.broadcasted_iota(jnp.int32, (1, n * rows), 1))
-    source = lax.broadcasted_iota(jnp.int32, (rows, 1), 0)
-    keep = jnp.where((col_source == source) & (col_owner == me), 1.0, 0.0).astype(bf16)
 
     def target(k):
         return lax.rem(z + k, line)
@@ -434,7 +428,28 @@
                 + y_in[here, cols].astype(f32)
             ).astype(bf16)
             reduce_z[k - 1][cut].start()
-    residual = jnp.dot(keep, x_all[:, :feat], preferred_element_type=f32)
+    for load in loads[4:8]:
+        load.wait()
+    before = context.shape[0]
+    horizon = frame_offset.shape[0]
+    for f in range(horizon):
+        voice = jnp.zeros((rows, width), f32)
+        for t in range(taps.shape[0]):
+            tap = taps[t : t + 1, :]
+            if f + t < before:
+                voice = voice + tap * context[f + t].astype(f32)
+            else:
+                voice = voice + tap * frame_offset[f + t - before : f + t - before + 1, :]
+        base_voice[f] = voice
+        gains[f : f + 1, :] = jnp.sum(taps[before - f :, :], axis=0, keepdims=True)
+
+    diagonal = lax.broadcasted_iota(jnp.int32, (rows, rows), 0) == lax.broadcasted_iota(
+        jnp.int32, (rows, rows), 1
+    )
+    count = jnp.sum(
+        jnp.where(diagonal, count_ref[...].astype(f32), 0.0), axis=1, keepdims=True
+    )
+    residual = jnp.dot(keep[...], x_all[:, :feat], preferred_element_type=f32)
     for cut in range(cuts):
         reduce_y[0][cut].wait_recv()
     total = (
@@ -452,19 +467,12 @@
     normed = (hidden * scale).astype(bf16)
 
     loads[11].wait()
-    diagonal = lax.broadcasted_iota(jnp.int32, (rows, rows), 0) == lax.broadcasted_iota(
-        jnp.int32, (rows, rows), 1
-    )
-    count = jnp.sum(
-        jnp.where(diagonal, count_ref[...].astype(f32), 0.0), axis=1, keepdims=True
-    )
     for j in range(width // tile):
         cols = slice(j * tile, (j + 1) * tile)
         talk = jnp.dot(normed, proj[:, cols], preferred_element_type=f32)
         owned = talk.astype(bf16).astype(f32)
         for f in range(horizon):
-            gain = jnp.sum(taps[before - f :, cols], axis=0, keepdims=True)
-            voice = base_voice[f, :, cols] + gain * owned
+            voice = base_voice[f, :, cols] + gains[f : f + 1, cols] * owned
             voices[:, f, cols] = jnp.where(count > f, voice, 0.0)
         voice_ref[:, :, cols] = voices[:, :, cols].astype(bf16)
 
@@ -523,6 +531,9 @@
             pltpu.VMEM((horizon, width), f32),
             pltpu.VMEM(conv_weight.shape, f32),
             pltpu.VMEM((horizon, rows, width), f32),
+            pltpu.VMEM((horizon, width), f32),
+            pltpu.VMEM((every, every), bf16),
+            pltpu.VMEM((rows, every), bf16),
             pltpu.VMEM((rows, horizon, width), f32),
             pltpu.VMEM((feat, hid), bf16),
             pltpu.VMEM((feat, hid), bf16),

time: 34.1 us -> 34.1 us (level)
  no operation moved by 1% of the time
where the time goes in v7:
time: 34.1 us; the launch traced here: 34 us
  Pallas kernels  32.3 us (95%)
  local copies, waits for them, and re-layouts  1.61 us (5%)
    pallas_call x1, Pallas kernels, dense_path(): pl.pallas_call(functools.partial(dense_kernel, n), out_shape=jax.ShapeDty...  32.3 us
    unnamed x1, local copies, waits for them, and re-layouts  1.61 us

profile of v7, /device:TPU:0, one launch (start us, length us, event | category | flops | bytes accessed | tf_op | source)
XLA Modules:
  0.0 34.0 jit_solution(17029575609275679268)
XLA Ops:
  0.0 32.3 %shard_map.118 = bf16[16,4,1024]{2,1,0:T(4,128)(2,1)} custom-call(bf16[16,2048]{1,0:T(8,128)(2,1)} %rows_hbm.1, s32[8,16]{1,0:T(8,128)} %bitcast.5, f32[8,16]{1,0:T(8,128)} %bitcast.6, s32[1,16]{1,0:T(1,128)} %slot_hbm.1, s32[1,16]{1,0:T(1,128)} %bitcast.7, bf16[6,16,1024]{2,1,0:T(8,128)(2,1)} %bitcast.4, f32[4,1024]{1,0:T(4,128)} %offset_hbm.1, ...), custom_call_target="tpu_custom_call" | custom-call | tf_op jit(solution)/shard_map/pallas_call | solution.py:519
  32.4 1.6 %copy.14 = bf16[16,4,1024]{2,1,0:T(4,128)(2,1)} copy(bf16[16,4,1024]{2,1,0:T(4,128)(2,1)} %shard_map.118) | data formatting | bytes 262144

commit v8 on v7

--- a/solution.py
+++ b/solution.py
@@ -198,6 +198,9 @@
     for peer in partners:
         pl.semaphore_signal(barrier, inc=1, device_id={"ep": peer})
 
+    for load in loads[8:10]:
+        load.start()
+
     extra = x_all.shape[1] - feat
     spot = lax.broadcasted_iota(jnp.int32, (extra, rows), 0)
     expert_of = lax.rem(spot, n)
@@ -291,7 +294,7 @@
     hand_on(z)
     for d in range(2, line):
         to_z(d, lambda copy: copy.start())
-    for load in loads[4:]:
+    for load in loads[4:8]:
         load.start()
 
     order[...] = regroup()
@@ -303,6 +306,7 @@
         if d < line - 1:
             at_distance(d - 1, from_y)
 
+    loads[10].start()
     loads[8].wait()
     loads[9].wait()
 
@@ -366,6 +370,7 @@
     up_pass(2 * half, 0, steps)
     grouped[...] = jnp.dot(order[...], inner[...], preferred_element_type=f32).astype(bf16)
     loads[10].wait()
+    loads[11].start()
     for cut in range(cuts):
         down_pass(2 * half, cut)
         reduce_s[1][cut].start()

time: 34.1 us -> 34.1 us (level)
  no operation moved by 1% of the time
where the time goes in v8:
time: 34.1 us; the launch traced here: 33.9 us
  Pallas kernels  32.3 us (95%)
  local copies, waits for them, and re-layouts  1.61 us (5%)
    pallas_call x1, Pallas kernels, dense_path(): pl.pallas_call(functools.partial(dense_kernel, n), out_shape=jax.ShapeDty...  32.3 us
    unnamed x1, local copies, waits for them, and re-layouts  1.61 us

profile of v8, /device:TPU:0, one launch (start us, length us, event | category | flops | bytes accessed | tf_op | source)
XLA Modules:
  0.0 33.9 jit_solution(12548582576001827128)
XLA Ops:
  0.0 32.3 %shard_map.118 = bf16[16,4,1024]{2,1,0:T(4,128)(2,1)} custom-call(bf16[16,2048]{1,0:T(8,128)(2,1)} %rows_hbm.1, s32[8,16]{1,0:T(8,128)} %bitcast.5, f32[8,16]{1,0:T(8,128)} %bitcast.6, s32[1,16]{1,0:T(1,128)} %slot_hbm.1, s32[1,16]{1,0:T(1,128)} %bitcast.7, bf16[6,16,1024]{2,1,0:T(8,128)(2,1)} %bitcast.4, f32[4,1024]{1,0:T(4,128)} %offset_hbm.1, ...), custom_call_target="tpu_custom_call" | custom-call | tf_op jit(solution)/shard_map/pallas_call | solution.py:524
  32.3 1.6 %copy.14 = bf16[16,4,1024]{2,1,0:T(4,128)(2,1)} copy(bf16[16,4,1024]{2,1,0:T(4,128)(2,1)} %shard_map.118) | data formatting | bytes 262144

commit v9 on v5

--- a/solution.py
+++ b/solution.py
@@ -504,7 +504,7 @@
     chosen = expert_ids.shape[1]
     before = left_context.shape[1]
     horizon = frame_offset.shape[0]
-    cuts = 2
+    cuts = 4
     vmem = pl.BlockSpec(memory_space=pltpu.VMEM)
     hbm = pl.BlockSpec(memory_space=pl.ANY)
     dma = pltpu.SemaphoreType.DMA

time: 34.1 us -> 34.4 us (level)
  no operation moved by 1% of the time
where the time goes in v9:
time: 34.4 us; the launch traced here: 34.2 us
  Pallas kernels  32.6 us (95%)
  local copies, waits for them, and re-layouts  1.61 us (5%)
    pallas_call x1, Pallas kernels, dense_path(): pl.pallas_call(functools.partial(dense_kernel, n), out_shape=jax.ShapeDty...  32.6 us
    unnamed x1, local copies, waits for them, and re-layouts  1.61 us

profile of v9, /device:TPU:0, one launch (start us, length us, event | category | flops | bytes accessed | tf_op | source)
XLA Modules:
  0.0 34.2 jit_solution(8059573163766614769)
XLA Ops:
  0.0 32.6 %shard_map.118 = bf16[16,4,1024]{2,1,0:T(4,128)(2,1)} custom-call(bf16[16,2048]{1,0:T(8,128)(2,1)} %rows_hbm.1, s32[8,16]{1,0:T(8,128)} %bitcast.5, f32[8,16]{1,0:T(8,128)} %bitcast.6, s32[1,16]{1,0:T(1,128)} %slot_hbm.1, s32[1,16]{1,0:T(1,128)} %bitcast.7, bf16[6,16,1024]{2,1,0:T(8,128)(2,1)} %bitcast.4, f32[4,1024]{1,0:T(4,128)} %offset_hbm.1, ...), custom_call_target="tpu_custom_call" | custom-call | tf_op jit(solution)/shard_map/pallas_call | solution.py:511
  32.6 1.6 %copy.14 = bf16[16,4,1024]{2,1,0:T(4,128)(2,1)} copy(bf16[16,4,1024]{2,1,0:T(4,128)(2,1)} %shard_map.118) | data formatting | bytes 262144
